TPU v7x, 512 devices: a whole 4x4x16 slice. The times are simulated.
512 devices in a mesh: rows: 4 (over y), ctx: 16 (over z), expert: 8 (over x, core).
Axes of the slice: x: 4, y: 4, z: 16, core: 2. Of those that a mesh axis runs over, the one named last changes fastest.
Arguments:
- queries: bfloat16 [32, 24, 128], P('expert', 'rows'), may hold values from -6 to 6
- cache_keys: bfloat16 [32, 4, 2048, 128], P('expert', 'rows', 'ctx'), may hold values from -6 to 6
- cache_values: bfloat16 [32, 4, 2048, 128], P('expert', 'rows', 'ctx'), may hold values from -96 to 96
- residual: bfloat16 [32, 3072], P('expert', 'rows'), may hold values from -1.5 to 1.5
- lengths: int32 [32], P('expert'), may hold values from 1 to 2048, as said below
- expert_ids: int32 [32, 2], P('expert'), may hold values from 0 to 7, all different within a row; in each aligned block of 4 rows (0 to 3, 4 to 7, ...) at most 2 rows name the same one
- router: float32 [3072, 8], replicated, may hold values from -0.109375 to 0.109375
- gate_weight: bfloat16 [8, 3072, 16384], P('expert', None, ('rows', 'ctx')), may hold values from -0.109375 to 0.109375
- up_weight: bfloat16 [8, 3072, 16384], P('expert', None, ('rows', 'ctx')), may hold values from -0.109375 to 0.109375
- down_weight: bfloat16 [8, 16384, 3072], P('expert', ('rows', 'ctx')), may hold values from -0.125 to 0.125
Outputs:
- mixed: bfloat16 [32, 3072], P('expert', ('rows', 'ctx'))
Inputs may be any that keep to these rules, and one draw needn't show every extreme that they name: `expert_ids`: within each aligned block of 4 rows (the rows of one device along expert) no expert is named by more than 2 rows, a bound that some block reaches; the two experts of a row differ, and every expert is named somewhere. `lengths`: at least a quarter of the rows have length 2048.
All inputs are finite; a program needn't handle non-finite values.
Results may differ from a plain program's by a relative error of at most 0.0069.
Values may be sent and summed in bfloat16 or wider, within the bound.
No kernel may reach another device: no remote copies, remote signals or barrier semaphores. Data moves between devices by JAX's collectives and lax.ppermute only.
A program may use at most 64 MiB of HBM per device.

v0:
```python
import math

import jax
import jax.numpy as jnp
from jax import lax
from jax.sharding import PartitionSpec as P

ITERS = 12


def local_mass(scaled, usable, middle):
    excess = jnp.maximum(scaled - middle, 0.0)
    return jnp.sum(jnp.where(usable, excess * excess, 0.0), axis=-1, keepdims=True)


def body(
    queries,
    cache_keys,
    cache_values,
    residual,
    lengths,
    expert_ids,
    router,
    gate_weight,
    up_weight,
    down_weight,
):
    rows_here, head_dev, head_size = queries.shape
    kv_dev = cache_keys.shape[1]
    ctx_here = cache_keys.shape[2]
    groups = head_dev // kv_dev
    factor = 0.5 / math.sqrt(head_size)
    grouped = queries.reshape(rows_here, kv_dev, groups, head_size)
    raw = jnp.einsum("rkgd,rkcd->rkgc", grouped, cache_keys, preferred_element_type=jnp.float32)
    scaled = raw * factor
    position = lax.axis_index("ctx") * ctx_here + jnp.arange(ctx_here, dtype=jnp.int32)
    usable = position[None, None, None, :] < lengths[:, None, None, None]
    local_top = jnp.max(jnp.where(usable, scaled, -1e30), axis=-1, keepdims=True)
    top_score = lax.pmax(local_top, "ctx")
    key_count = lengths.astype(jnp.float32)[:, None, None, None]
    low_end = top_score - 1.0
    high_end = top_score - 1.0 / jnp.sqrt(key_count)
    interval = high_end - low_end
    start_state = (low_end, interval, low_end, jnp.ones_like(low_end))

    def one_round(round_index, carried):
        low_now, width_now, middle_now, total_now = carried
        width_now = width_now / 2.0
        middle_now = low_now + width_now
        total_now = lax.psum(local_mass(scaled, usable, middle_now), "ctx")
        low_now = jnp.where(total_now >= 1.0, middle_now, low_now)
        return (low_now, width_now, middle_now, total_now)

    final_state = lax.fori_loop(0, ITERS, one_round, start_state)
    middle = final_state[2]
    total = final_state[3]
    excess = jnp.maximum(scaled - middle, 0.0)
    weights = jnp.where(usable, excess * excess, 0.0).astype(jnp.bfloat16)
    partial_value = jnp.einsum(
        "rkgc,rkcd->rkgd", weights, cache_values, preferred_element_type=jnp.float32
    )
    summed_heads = lax.psum(partial_value, "ctx")
    attended = (summed_heads / total).reshape(rows_here, -1)
    hidden_part = (residual.astype(jnp.float32) + attended).astype(jnp.bfloat16)
    hidden = lax.all_gather(hidden_part, "rows", axis=1, tiled=True)
    model_width = hidden.shape[1]
    expert_total = router.shape[1]
    logits = jnp.dot(hidden.astype(jnp.float32), router, precision=lax.Precision.HIGHEST)
    expert_iota = jnp.arange(expert_total, dtype=jnp.int32)
    picked = expert_ids[:, :, None] == expert_iota[None, None, :]
    chosen = jnp.sum(jnp.where(picked, logits[:, None, :], 0.0), axis=-1)
    first_share = 1.0 / (1.0 + jnp.exp(chosen[:, 1] - chosen[:, 0]))
    second_share = 1.0 / (1.0 + jnp.exp(chosen[:, 0] - chosen[:, 1]))
    shares = jnp.stack([first_share, second_share], axis=1)
    capacity = rows_here // 2
    flat_ids = expert_ids.reshape(-1)
    onehot = (flat_ids[:, None] == expert_iota[None, :]).astype(jnp.int32)
    before = jnp.cumsum(onehot, axis=0) - onehot
    slot_index = jnp.sum(onehot * before, axis=1)
    target = (flat_ids * capacity + slot_index).reshape(rows_here, 2)
    slots_iota = jnp.arange(expert_total * capacity, dtype=jnp.int32)
    matches = slots_iota[:, None, None] == target[None, :, :]
    placing = jnp.sum(matches.astype(jnp.int32), axis=2).astype(jnp.bfloat16)
    outgoing = jnp.dot(placing, hidden, preferred_element_type=jnp.float32).astype(jnp.bfloat16)
    outgoing = outgoing.reshape(expert_total, capacity, model_width)
    gathered = lax.all_to_all(outgoing, "expert", split_axis=0, concat_axis=0, tiled=True)
    sources = lax.axis_size("expert")
    local_count = gate_weight.shape[0]
    arrived = gathered.reshape(sources, local_count, capacity, model_width)
    gate_act = jnp.einsum(
        "secd,edf->secf", arrived, gate_weight, preferred_element_type=jnp.float32
    )
    up_act = jnp.einsum("secd,edf->secf", arrived, up_weight, preferred_element_type=jnp.float32)
    product = (jax.nn.silu(gate_act) * up_act).astype(jnp.bfloat16)
    partial_out = jnp.einsum(
        "secf,efd->secd", product, down_weight, preferred_element_type=jnp.float32
    )
    blending = jnp.sum(jnp.where(matches, shares[None, :, :], 0.0), axis=2).T
    summed = lax.psum_scatter(partial_out, ("rows", "ctx"), scatter_dimension=3, tiled=True)
    returned_rows = lax.all_to_all(summed, "expert", split_axis=0, concat_axis=0, tiled=True)
    returned_rows = returned_rows.reshape(expert_total * capacity, -1)
    mixed_part = jnp.dot(blending, returned_rows, precision=lax.Precision.HIGHEST)
    slice_width = mixed_part.shape[1]
    slice_start = lax.axis_index(("rows", "ctx")) * slice_width
    base_rows = lax.dynamic_slice_in_dim(hidden, slice_start, slice_width, 1)
    return (base_rows.astype(jnp.float32) + mixed_part).astype(jnp.bfloat16)


def solution(mesh):
    placed = (
        P("expert", "rows", None),
        P("expert", "rows", "ctx", None),
        P("expert", "rows", "ctx", None),
        P("expert", "rows"),
        P("expert"),
        P("expert", None),
        P(),
        P("expert", None, ("rows", "ctx")),
        P("expert", None, ("rows", "ctx")),
        P("expert", ("rows", "ctx"), None),
    )
    return jax.shard_map(
        body, mesh=mesh, in_specs=placed, out_specs=P("expert", ("rows", "ctx")), check_vma=False
    )
```

profile of v0, /device:TPU:1, one launch (start us, length us, event | category | flops | bytes accessed | tf_op | source)
XLA Modules:
  0.0 1199.1 jit_solution(7287698741852597815)
XLA Ops:
  6.5 0.8 convert_rsqrt_fusion
  7.3 0.7 broadcast_compare_fusion
  8.1 1.2 select_reduce_fusion.1
  9.2 30.5 %pmax.7 = f32[4,1,6,1]{2,0,3,1:T(4,128)S(1)} all-reduce(f32[4,1,6,1]{2,0,3,1:T(4,128)S(1)} %bitcast.106), channel_id=1, replica_groups=mesh['rows'=4,'ctx'=16,'expert'=8] {'ctx'}, use_global_device_ids=true, to_apply=%region_1.2 | all-reduce | flops 24 | bytes 192 | tf_op jit(solution)/shard_map/pmax | solution.py:39
  39.8 0.6 copy.57
  40.4 267.7 %while.17 = (s32[]{:T(128)}, f32[4,1,6,1]{2,0,3,1:T(4,128)S(1)}, f32[4,1,6,1]{2,0,3,1:T(4,128)S(1)}, f32[4,1,6,1]{2,0,3,1:T(4,128)}, f32[4,1,6,1]{2,0,3,1:T(4,12...) while((s32[]{:T(128)}, f32[4,1,6,1]{2,0,3,1:T(4,128)S(1)}, ...), condition=%wide.region_5.6_spmd.clone, body=%wide.region_2.5_spmd.clone.sunk | while | flops 15970 | bytes 15909 | solution.py:54
  40.4 0.7 compare_bitcast_fusion.2
  41.3 20.0 %psum.17 = f32[4,1,6,1]{2,0,3,1:T(4,128)S(1)} all-reduce(f32[4,1,6,1]{2,0,3,1:T(4,128)S(1)} %bitcast.102), channel_id=1, replica_groups=mesh['rows'=4,'ctx'=16,'expert'=8] {'ctx'}, use_global_device_ids=true, to_apply=%region_4.4 | all-reduce | flops 24 | bytes 192 | tf_op jit(solution)/shard_map/while/body/eval_jaxpr/psum | solution.py:50
  61.3 0.6 copy-done.3
  61.9 0.7 compare_bitcast_fusion.2
  62.8 21.5 %psum.17 = f32[4,1,6,1]{2,0,3,1:T(4,128)S(1)} all-reduce(f32[4,1,6,1]{2,0,3,1:T(4,128)S(1)} %bitcast.102), channel_id=1, replica_groups=mesh['rows'=4,'ctx'=16,'expert'=8] {'ctx'}, use_global_device_ids=true, to_apply=%region_4.4 | all-reduce | flops 24 | bytes 192 | tf_op jit(solution)/shard_map/while/body/eval_jaxpr/psum | solution.py:50
  84.3 0.6 copy-done.3
  84.9 0.7 compare_bitcast_fusion.2
  85.8 20.6 %psum.17 = f32[4,1,6,1]{2,0,3,1:T(4,128)S(1)} all-reduce(f32[4,1,6,1]{2,0,3,1:T(4,128)S(1)} %bitcast.102), channel_id=1, replica_groups=mesh['rows'=4,'ctx'=16,'expert'=8] {'ctx'}, use_global_device_ids=true, to_apply=%region_4.4 | all-reduce | flops 24 | bytes 192 | tf_op jit(solution)/shard_map/while/body/eval_jaxpr/psum | solution.py:50
  106.4 0.6 copy-done.3
  107.0 0.7 compare_bitcast_fusion.2
  107.8 21.0 %psum.17 = f32[4,1,6,1]{2,0,3,1:T(4,128)S(1)} all-reduce(f32[4,1,6,1]{2,0,3,1:T(4,128)S(1)} %bitcast.102), channel_id=1, replica_groups=mesh['rows'=4,'ctx'=16,'expert'=8] {'ctx'}, use_global_device_ids=true, to_apply=%region_4.4 | all-reduce | flops 24 | bytes 192 | tf_op jit(solution)/shard_map/while/body/eval_jaxpr/psum | solution.py:50
  128.8 0.6 copy-done.3
  129.4 0.7 compare_bitcast_fusion.2
  130.3 20.6 %psum.17 = f32[4,1,6,1]{2,0,3,1:T(4,128)S(1)} all-reduce(f32[4,1,6,1]{2,0,3,1:T(4,128)S(1)} %bitcast.102), channel_id=1, replica_groups=mesh['rows'=4,'ctx'=16,'expert'=8] {'ctx'}, use_global_device_ids=true, to_apply=%region_4.4 | all-reduce | flops 24 | bytes 192 | tf_op jit(solution)/shard_map/while/body/eval_jaxpr/psum | solution.py:50
  150.9 0.6 copy-done.3
  151.5 0.7 compare_bitcast_fusion.2
  152.4 21.3 %psum.17 = f32[4,1,6,1]{2,0,3,1:T(4,128)S(1)} all-reduce(f32[4,1,6,1]{2,0,3,1:T(4,128)S(1)} %bitcast.102), channel_id=1, replica_groups=mesh['rows'=4,'ctx'=16,'expert'=8] {'ctx'}, use_global_device_ids=true, to_apply=%region_4.4 | all-reduce | flops 24 | bytes 192 | tf_op jit(solution)/shard_map/while/body/eval_jaxpr/psum | solution.py:50
  173.7 0.6 copy-done.3
  174.2 0.7 compare_bitcast_fusion.2
  175.1 20.6 %psum.17 = f32[4,1,6,1]{2,0,3,1:T(4,128)S(1)} all-reduce(f32[4,1,6,1]{2,0,3,1:T(4,128)S(1)} %bitcast.102), channel_id=1, replica_groups=mesh['rows'=4,'ctx'=16,'expert'=8] {'ctx'}, use_global_device_ids=true, to_apply=%region_4.4 | all-reduce | flops 24 | bytes 192 | tf_op jit(solution)/shard_map/while/body/eval_jaxpr/psum | solution.py:50
  195.8 0.6 copy-done.3
  196.3 0.7 compare_bitcast_fusion.2
  197.2 20.9 %psum.17 = f32[4,1,6,1]{2,0,3,1:T(4,128)S(1)} all-reduce(f32[4,1,6,1]{2,0,3,1:T(4,128)S(1)} %bitcast.102), channel_id=1, replica_groups=mesh['rows'=4,'ctx'=16,'expert'=8] {'ctx'}, use_global_device_ids=true, to_apply=%region_4.4 | all-reduce | flops 24 | bytes 192 | tf_op jit(solution)/shard_map/while/body/eval_jaxpr/psum | solution.py:50
  218.2 0.6 copy-done.3
  218.7 0.7 compare_bitcast_fusion.2
  219.6 20.6 %psum.17 = f32[4,1,6,1]{2,0,3,1:T(4,128)S(1)} all-reduce(f32[4,1,6,1]{2,0,3,1:T(4,128)S(1)} %bitcast.102), channel_id=1, replica_groups=mesh['rows'=4,'ctx'=16,'expert'=8] {'ctx'}, use_global_device_ids=true, to_apply=%region_4.4 | all-reduce | flops 24 | bytes 192 | tf_op jit(solution)/shard_map/while/body/eval_jaxpr/psum | solution.py:50
  240.3 0.6 copy-done.3
  240.9 0.7 compare_bitcast_fusion.2
  241.7 21.2 %psum.17 = f32[4,1,6,1]{2,0,3,1:T(4,128)S(1)} all-reduce(f32[4,1,6,1]{2,0,3,1:T(4,128)S(1)} %bitcast.102), channel_id=1, replica_groups=mesh['rows'=4,'ctx'=16,'expert'=8] {'ctx'}, use_global_device_ids=true, to_apply=%region_4.4 | all-reduce | flops 24 | bytes 192 | tf_op jit(solution)/shard_map/while/body/eval_jaxpr/psum | solution.py:50
  263.0 0.6 copy-done.3
  263.6 0.7 compare_bitcast_fusion.2
  264.5 20.6 %psum.17 = f32[4,1,6,1]{2,0,3,1:T(4,128)S(1)} all-reduce(f32[4,1,6,1]{2,0,3,1:T(4,128)S(1)} %bitcast.102), channel_id=1, replica_groups=mesh['rows'=4,'ctx'=16,'expert'=8] {'ctx'}, use_global_device_ids=true, to_apply=%region_4.4 | all-reduce | flops 24 | bytes 192 | tf_op jit(solution)/shard_map/while/body/eval_jaxpr/psum | solution.py:50
  285.1 0.6 copy-done.3
  285.7 0.7 compare_bitcast_fusion.2
  286.6 20.9 %psum.17 = f32[4,1,6,1]{2,0,3,1:T(4,128)S(1)} all-reduce(f32[4,1,6,1]{2,0,3,1:T(4,128)S(1)} %bitcast.102), channel_id=1, replica_groups=mesh['rows'=4,'ctx'=16,'expert'=8] {'ctx'}, use_global_device_ids=true, to_apply=%region_4.4 | all-reduce | flops 24 | bytes 192 | tf_op jit(solution)/shard_map/while/body/eval_jaxpr/psum | solution.py:50
  307.5 0.6 copy-done.3
  308.1 1.1 convolution_bitcast_fusion.1
  309.2 39.4 %psum.14 = f32[4,1,6,128]{3,2,0,1:T(8,128)S(1)} all-reduce(f32[4,1,6,128]{3,2,0,1:T(8,128)S(1)} %convolution_bitcast_fusion.1), channel_id=1, replica_groups=mesh['rows'=4,'ctx'=16,'expert'=8] {'ctx'}, use_global_device_ids=true, to_apply=%region_6.7 | all-reduce | flops 3072 | bytes 24576 | tf_op jit(solution)/shard_map/psum | solution.py:62
  348.6 0.7 divide_bitcast_fusion
  349.4 0.7 fusion.35
  350.1 9.7 all_gather.3
  359.8 0.8 copy.34
  361.2 0.2 convolution_convert_fusion
  361.4 0.7 reshape.157
  362.1 114.2 %all-to-all-start = ((bf16[8,2,3072]{2,1,0:T(2,128)(2,1)}), bf16[8,2,3072]{2,1,0:T(2,128)(2,1)S(1)}, u32[]{:S(2)}, u32[]{:S(2)}) async-start(bf16[8,2,3072]{2,1,0:T(2,128)(2,1)} %reshape.157), calls=%async_computation | async-start | bytes 196608 | tf_op jit(solution)/shard_map/all_to_all | solution.py:86
  476.2 1.1 fusion.46
  477.3 3.9 all-to-all-done
  481.2 1.7 fusion.7
  482.9 1.0 convolution_bitcast_fusion
  483.9 3.3 copy.40
  487.3 4.3 reshape.166
  491.6 0.7 copy-done.4
  492.4 676.9 %reduce-scatter.4.cloned.1.call-done = f32[48,16]{1,0:T(8,128)} async-done(((f32[3072,16]{1,0:T(8,128)}), f32[48,16]{1,0:T(8,128)}) %reduce-scatter.4.cloned.1.call-update) | async-done | bytes 3088
  1169.3 0.8 reshape.167
  1170.2 0.7 copy.39
  1170.8 16.1 %all-to-all-start.1 = ((f32[8,1,2,48]{3,2,1,0:T(2,128)}), f32[8,1,2,48]{3,2,1,0:T(2,128)S(1)}, u32[]{:S(2)}, u32[]{:S(2)}) async-start(f32[8,1,2,48]{3,2,1,0:T(2,128)} %copy.39), calls=%async_computation.1 | async-start | bytes 16384 | tf_op jit(solution)/shard_map/all_to_all | solution.py:100
  1187.0 4.5 all-to-all-done.1
  1191.5 0.7 fusion.22
  (94 shorter events, 3.2 us)
Async XLA Ops:
  6.5 476.4 %copy-start = (bf16[1,256,3072]{2,1,0:T(8,128)(2,1)S(1)}, bf16[1,256,3072]{2,1,0:T(8,128)(2,1)}, u32[]{:S(2)}) copy-start(bf16[1,256,3072]{2,1,0:T(8,128)(2,1)} %param.21) | copy-start | bytes 4718596
  9.2 473.7 %copy-start.1 = (bf16[1,3072,256]{2,1,0:T(8,128)(2,1)S(1)}, bf16[1,3072,256]{2,1,0:T(8,128)(2,1)}, u32[]{:S(2)}) copy-start(bf16[1,3072,256]{2,1,0:T(8,128)(2,1)} %param.20) | copy-start | bytes 4718596
  40.4 21.0 %copy-start.2 = (f32[4,1,6,1]{2,0,3,1:T(4,128)}, f32[4,1,6,1]{2,0,3,1:T(4,128)S(1)}, u32[]{:S(2)}) copy-start(f32[4,1,6,1]{2,0,3,1:T(4,128)S(1)} %get-tuple-element.187) | copy-start | bytes 292 | tf_op jit(solution)/shard_map/while
  61.3 0.6 copy-start.3
  61.9 22.4 %copy-start.2 = (f32[4,1,6,1]{2,0,3,1:T(4,128)}, f32[4,1,6,1]{2,0,3,1:T(4,128)S(1)}, u32[]{:S(2)}) copy-start(f32[4,1,6,1]{2,0,3,1:T(4,128)S(1)} %get-tuple-element.187) | copy-start | bytes 292 | tf_op jit(solution)/shard_map/while
  84.3 0.6 copy-start.3
  84.9 21.5 %copy-start.2 = (f32[4,1,6,1]{2,0,3,1:T(4,128)}, f32[4,1,6,1]{2,0,3,1:T(4,128)S(1)}, u32[]{:S(2)}) copy-start(f32[4,1,6,1]{2,0,3,1:T(4,128)S(1)} %get-tuple-element.187) | copy-start | bytes 292 | tf_op jit(solution)/shard_map/while
  106.4 0.6 copy-start.3
  107.0 21.9 %copy-start.2 = (f32[4,1,6,1]{2,0,3,1:T(4,128)}, f32[4,1,6,1]{2,0,3,1:T(4,128)S(1)}, u32[]{:S(2)}) copy-start(f32[4,1,6,1]{2,0,3,1:T(4,128)S(1)} %get-tuple-element.187) | copy-start | bytes 292 | tf_op jit(solution)/shard_map/while
  128.8 0.6 copy-start.3
  129.4 21.5 %copy-start.2 = (f32[4,1,6,1]{2,0,3,1:T(4,128)}, f32[4,1,6,1]{2,0,3,1:T(4,128)S(1)}, u32[]{:S(2)}) copy-start(f32[4,1,6,1]{2,0,3,1:T(4,128)S(1)} %get-tuple-element.187) | copy-start | bytes 292 | tf_op jit(solution)/shard_map/while
  150.9 0.6 copy-start.3
  151.5 22.2 %copy-start.2 = (f32[4,1,6,1]{2,0,3,1:T(4,128)}, f32[4,1,6,1]{2,0,3,1:T(4,128)S(1)}, u32[]{:S(2)}) copy-start(f32[4,1,6,1]{2,0,3,1:T(4,128)S(1)} %get-tuple-element.187) | copy-start | bytes 292 | tf_op jit(solution)/shard_map/while
  173.6 0.6 copy-start.3
  174.2 21.5 %copy-start.2 = (f32[4,1,6,1]{2,0,3,1:T(4,128)}, f32[4,1,6,1]{2,0,3,1:T(4,128)S(1)}, u32[]{:S(2)}) copy-start(f32[4,1,6,1]{2,0,3,1:T(4,128)S(1)} %get-tuple-element.187) | copy-start | bytes 292 | tf_op jit(solution)/shard_map/while
  195.7 0.6 copy-start.3
  196.3 21.8 %copy-start.2 = (f32[4,1,6,1]{2,0,3,1:T(4,128)}, f32[4,1,6,1]{2,0,3,1:T(4,128)S(1)}, u32[]{:S(2)}) copy-start(f32[4,1,6,1]{2,0,3,1:T(4,128)S(1)} %get-tuple-element.187) | copy-start | bytes 292 | tf_op jit(solution)/shard_map/while
  218.1 0.6 copy-start.3
  218.7 21.5 %copy-start.2 = (f32[4,1,6,1]{2,0,3,1:T(4,128)}, f32[4,1,6,1]{2,0,3,1:T(4,128)S(1)}, u32[]{:S(2)}) copy-start(f32[4,1,6,1]{2,0,3,1:T(4,128)S(1)} %get-tuple-element.187) | copy-start | bytes 292 | tf_op jit(solution)/shard_map/while
  240.3 0.6 copy-start.3
  240.9 22.2 %copy-start.2 = (f32[4,1,6,1]{2,0,3,1:T(4,128)}, f32[4,1,6,1]{2,0,3,1:T(4,128)S(1)}, u32[]{:S(2)}) copy-start(f32[4,1,6,1]{2,0,3,1:T(4,128)S(1)} %get-tuple-element.187) | copy-start | bytes 292 | tf_op jit(solution)/shard_map/while
  263.0 0.6 copy-start.3
  263.6 21.5 %copy-start.2 = (f32[4,1,6,1]{2,0,3,1:T(4,128)}, f32[4,1,6,1]{2,0,3,1:T(4,128)S(1)}, u32[]{:S(2)}) copy-start(f32[4,1,6,1]{2,0,3,1:T(4,128)S(1)} %get-tuple-element.187) | copy-start | bytes 292 | tf_op jit(solution)/shard_map/while
  285.1 0.6 copy-start.3
  285.7 21.8 %copy-start.2 = (f32[4,1,6,1]{2,0,3,1:T(4,128)}, f32[4,1,6,1]{2,0,3,1:T(4,128)S(1)}, u32[]{:S(2)}) copy-start(f32[4,1,6,1]{2,0,3,1:T(4,128)S(1)} %get-tuple-element.187) | copy-start | bytes 292 | tf_op jit(solution)/shard_map/while
  307.5 0.6 copy-start.3
  362.1 119.1 %all-to-all-start = ((bf16[8,2,3072]{2,1,0:T(2,128)(2,1)}), bf16[8,2,3072]{2,1,0:T(2,128)(2,1)S(1)}, u32[]{:S(2)}, u32[]{:S(2)}) async-start(bf16[8,2,3072]{2,1,0:T(2,128)(2,1)} %reshape.157), calls=%async_computation | async-start | bytes 196608 | tf_op jit(solution)/shard_map/all_to_all | solution.py:86
  476.2 693.1 %reduce-scatter.4.cloned.1.call-start = ((), (), s32[]{:S(2)}) async-start(), calls=%async_computation.3 | async-start | bytes 1597440
  491.6 0.7 copy-start.4
  1170.8 20.7 %all-to-all-start.1 = ((f32[8,1,2,48]{3,2,1,0:T(2,128)}), f32[8,1,2,48]{3,2,1,0:T(2,128)S(1)}, u32[]{:S(2)}, u32[]{:S(2)}) async-start(f32[8,1,2,48]{3,2,1,0:T(2,128)} %copy.39), calls=%async_computation.1 | async-start | bytes 16384 | tf_op jit(solution)/shard_map/all_to_all | solution.py:100
Sparse Core Ops, SparseCore 0:
  491.7 677.5 reduce-scatter.3
where the time goes:
time: 1200 us
  waiting for transfers between devices  685 us (57%)
  blocking collectives  329 us (27%)
  starting transfers between devices  130 us (11%)
  local copies, waits for them, and re-layouts  19 us (2%)
  other arithmetic  14.6 us (1%)
  between operations  13.4 us (1%)
    unnamed x2, waiting for transfers between devices  677 us
    psum x12, blocking collectives, one_round(): total_now = lax.psum(local_mass(scaled, usable, middle_now), 'ctx')  250 us
    all_to_all x1, starting transfers between devices, body(): lax.all_to_all(outgoing, 'expert', split_axis=0, concat_axis=0, tiled=True)  114 us
    psum x1, blocking collectives, body(): summed_heads = lax.psum(partial_value, 'ctx')  39.4 us
    pmax x1, blocking collectives, body(): top_score = lax.pmax(local_top, 'ctx')  30.5 us
  transfers between devices with their start and end apart: 3, of which 3 were waited for; matrix products, arithmetic and copies ran while one was open for 0% of the time, Pallas kernels for 0%

commit v1 on v0

v1 whole, which is shorter than its diff:
```python
import functools
import math

import jax
import jax.numpy as jnp
from jax import lax
from jax.experimental import pallas as pl
from jax.experimental.pallas import tpu as pltpu
from jax.sharding import PartitionSpec as P

ITERS = 12
VMEM = pl.BlockSpec(memory_space=pltpu.VMEM)
SMEM = pl.BlockSpec(memory_space=pltpu.SMEM)
F32 = jnp.float32
BF16 = jnp.bfloat16
NEG = -1e30
HBM = pl.BlockSpec(memory_space=pltpu.HBM)
NT = (((1,), (1,)), ((), ()))


def call(kernel, outs, *args, specs, out_spec=VMEM, scratch=(), limit=16 << 20):
    return pl.pallas_call(
        kernel,
        out_shape=outs,
        in_specs=specs,
        out_specs=jax.tree.map(lambda _: out_spec, outs),
        scratch_shapes=scratch,
        compiler_params=pltpu.CompilerParams(vmem_limit_bytes=limit),
        cost_estimate=pl.CostEstimate(flops=1 << 36, bytes_accessed=1 << 28, transcendentals=0),
    )(*args)


def iota(shape, dim):
    return lax.broadcasted_iota(jnp.int32, shape, dim)


def one_hot(mask):
    return jnp.where(mask, 1.0, 0.0).astype(BF16)


def parts_of(x, count):
    parts = []
    for _ in range(count):
        part = x.astype(BF16)
        parts.append(part)
        x = x - part.astype(F32)
    return parts


def score_kernel(
    heads, k_hbm, q_hbm, len_hbm, res_hbm, v_hbm, out_hbm, out_ref, k_ref, q_ref, len_ref, res_ref, v_ref, sems, out_sems
):
    pairs = ((k_hbm, k_ref), (q_hbm, q_ref), (len_hbm, len_ref), (res_hbm, res_ref), (v_hbm, v_ref))
    copies = [pltpu.make_async_copy(src, dst, sems.at[i]) for i, (src, dst) in enumerate(pairs)]
    for copy in copies:
        copy.start()
    n_b, here, size = k_ref.shape
    split = out_ref.shape[0] // n_b
    dims = size // split
    c = lax.axis_index("ctx")
    place = c * here + iota((8, here), 1)
    eye = one_hot(iota((size, size), 0) == iota((size, size), 1))
    diagonal = iota((8, here), 0) == iota((8, here), 1)
    head = iota((8, heads * n_b), 0)
    for copy in copies[:4]:
        copy.wait()
    q = q_ref[...]
    res = res_ref[...].astype(F32)
    odd = lax.rem(c, 2) == 1
    half = heads // 2
    tails = []
    for b in range(n_b):
        pick = one_hot((iota(head.shape, 1) == head * n_b + b) & (head < heads))
        q_b = jnp.dot(pick, q, preferred_element_type=F32).astype(BF16)
        scaled = lax.dot_general(q_b, k_ref[b], NT, preferred_element_type=F32) * (0.5 / math.sqrt(size))
        valid = place < len_ref[b]
        top = jnp.max(jnp.where(valid, scaled, NEG), axis=-1, keepdims=True)
        top = jnp.where(top > 0.5 * NEG, top.astype(BF16).astype(F32), 0.0)
        rows = [part.astype(F32)[0:heads] for part in parts_of(jnp.where(valid, scaled - top, NEG), 2)]
        rows.append(jnp.sum(jnp.where(diagonal, top, 0.0), axis=0, keepdims=True))
        for k in range(half):
            even_part, odd_part = (res[b:b + 1, h * size:(h + 1) * size] for h in (k, half + k))
            rows.append(jnp.where(odd, odd_part, even_part))
        tails.append(jnp.concatenate(rows, axis=0))
    copies[4].wait()
    out_copies = []
    for b in range(n_b):
        turned = lax.dot_general(eye, v_ref[b], NT, preferred_element_type=F32)
        for j in range(split):
            block = jnp.concatenate([turned[j * dims:(j + 1) * dims], tails[b]], axis=0)
            out_ref[b * split + j] = block.astype(BF16)
        cut = pl.ds(b * split, split)
        out_copies.append(pltpu.make_async_copy(out_ref.at[cut], out_hbm.at[cut], out_sems.at[b]))
        out_copies[b].start()
    for copy in out_copies:
        copy.wait()


def attend_kernel(heads, split, got_ref, out_ref):
    n_c, rows, here = got_ref.shape
    dims = rows - 16
    j = lax.axis_index("ctx") % split
    parts = got_ref[:, dims:].astype(F32)
    diagonal = iota((n_c, 8, here), 1) == iota((n_c, 8, here), 2)
    tops = jnp.sum(jnp.where(diagonal, parts[:, 2 * heads:2 * heads + 1], 0.0), axis=-1, keepdims=True)
    blank = jnp.full((8 - heads, here), NEG, F32)
    scores = [jnp.concatenate([parts[i, 0:heads] + parts[i, heads:2 * heads], blank], axis=0) for i in range(n_c)]
    scores = jnp.stack(scores) + tops
    count = jnp.sum(jnp.sum(jnp.where(scores > 0.5 * NEG, 1.0, 0.0), axis=0), axis=-1, keepdims=True)
    count = jnp.maximum(count, 1.0)
    top = jnp.max(jnp.max(scores, axis=0), axis=-1, keepdims=True)
    low = top - 1.0
    interval = (top - 1.0 / jnp.sqrt(count)) - low

    def mass(middle):
        excess = jnp.maximum(scores - middle[None], 0.0)
        return jnp.sum(jnp.sum(excess * excess, axis=0), axis=-1, keepdims=True)

    for _ in range(ITERS // 3):
        w1 = interval / 2.0
        w2 = w1 / 2.0
        w3 = w2 / 2.0
        m1 = low + w1
        m2 = (low + w2, m1 + w2)
        m3 = (low + w3, m2[0] + w3, m1 + w3, m2[1] + w3)
        t1, t2, t3 = mass(m1), [mass(m) for m in m2], [mass(m) for m in m3]
        c1 = t1 >= 1.0
        low = jnp.where(c1, m1, low)
        c2 = jnp.where(c1, t2[1], t2[0]) >= 1.0
        low = jnp.where(c2, jnp.where(c1, m2[1], m2[0]), low)
        middle = jnp.where(c1, jnp.where(c2, m3[3], m3[2]), jnp.where(c2, m3[1], m3[0]))
        total = jnp.where(c1, jnp.where(c2, t3[3], t3[2]), jnp.where(c2, t3[1], t3[0]))
        low = jnp.where(total >= 1.0, middle, low)
        interval = w3
    excess = jnp.maximum(scores - middle[None], 0.0)
    weights = excess * excess
    weights = jnp.concatenate([weights[i] for i in range(n_c)], axis=1).astype(BF16)
    values = jnp.concatenate([got_ref[i, 0:dims] for i in range(n_c)], axis=1)
    attended = lax.dot_general(weights, values, NT, preferred_element_type=F32) / total
    attended = jnp.concatenate([attended] * split, axis=1)
    res = [parts[i, 2 * heads + 1:] for i in range(2)]
    res = jnp.concatenate(res + [jnp.zeros((8 - heads, here), F32)], axis=0)
    mine = (iota(res.shape, 1) // dims == j) & (iota(res.shape, 0) < heads)
    piece = jnp.where(mine, res + attended, 0.0).astype(BF16)
    for i in range(n_c):
        out_ref[i] = piece


def hidden_kernel(got_ref, hid_ref, out_ref):
    n_c = got_ref.shape[0]
    rows, size = hid_ref.shape
    n_b = 4
    split = n_c // n_b
    got = got_ref[...].astype(F32)
    whole = []
    for b in range(n_b):
        row = got[b * split]
        for j in range(1, split):
            row = row + got[b * split + j]
        whole.append(row)
    whole = jnp.concatenate(whole, axis=0).astype(BF16)
    at, src = iota((rows, 8 * n_b), 0), iota((rows, 8 * n_b), 1)
    pick = one_hot(src == (at % n_b) * 8 + at // n_b)
    hidden = jnp.dot(pick, whole, preferred_element_type=F32).astype(BF16)
    hid_ref[...] = hidden
    for i in range(out_ref.shape[0]):
        out_ref[i] = hidden


def expert_kernel(
    ids_ref, g_ref, router_ref, gate_ref, up_ref, down_ref, out_ref, share_ref, wide_ref
):
    n_r, n_e, block, _ = out_ref.shape
    n_b = 4
    rows = n_e * n_b
    heads = block // n_b
    width = heads * 128
    at, src = iota((heads * rows, n_e * block), 0), iota((heads * rows, n_e * block), 1)
    inner = at % rows
    pick = one_hot(src == (inner // n_b) * block + (at // rows) * n_b + inner % n_b)
    own = one_hot(iota((block, rows), 1) == lax.axis_index("expert") * n_b + iota((block, rows), 0) % n_b)
    routers = parts_of(router_ref[...], 3)
    gate = up = logits = None
    for r in range(n_r):
        moved = jnp.dot(pick, g_ref[r], preferred_element_type=F32).astype(BF16)
        x = jnp.concatenate([moved[h * rows:(h + 1) * rows] for h in range(heads)], axis=1)
        cols = slice(r * width, (r + 1) * width)
        g = jnp.dot(x, gate_ref[cols], preferred_element_type=F32)
        u = jnp.dot(x, up_ref[cols], preferred_element_type=F32)
        x_own = jnp.dot(own, x, preferred_element_type=F32).astype(BF16)
        hi, mid, low = [lax.dot_general(x_own, m[:, cols], NT, preferred_element_type=F32) for m in routers]
        l = (low + mid) + hi
        gate, up, logits = (g, u, l) if r == 0 else (gate + g, up + u, logits + l)
    act = ((gate / (1.0 + jnp.exp(-gate))) * up).astype(BF16)
    for r in range(n_r):
        o = jnp.dot(act, down_ref[:, r * width:(r + 1) * width], preferred_element_type=F32)
        for h in range(heads):
            piece = o[:, h * 128:(h + 1) * 128]
            for e in range(n_e):
                wide_ref[r, e, h * n_b:(h + 1) * n_b, :] = piece[e * n_b:(e + 1) * n_b]
    out_ref[...] = wide_ref[...].astype(BF16)
    which = iota(logits.shape, 1)
    owner = iota(logits.shape, 0) % n_b
    first = second = jnp.zeros(logits.shape, jnp.int32)
    for b in range(n_b):
        first = jnp.where(owner == b, ids_ref[0, b], first)
        second = jnp.where(owner == b, ids_ref[1, b], second)
    l0 = jnp.sum(jnp.where(which == first, logits, 0.0), axis=-1, keepdims=True)
    l1 = jnp.sum(jnp.where(which == second, logits, 0.0), axis=-1, keepdims=True)
    s0 = 1.0 / (1.0 + jnp.exp(l1 - l0))
    s1 = 1.0 / (1.0 + jnp.exp(l0 - l1))
    share_ref[...] = jnp.where(which == first, s0, 0.0) + jnp.where(which == second, s1, 0.0)


def split_kernel(width, parts_ref, share_ref, hid_ref, out_ref):
    n_c, n_b, _ = out_ref.shape
    n_e = share_ref.shape[1]
    n_r = parts_ref.shape[0] // n_e
    total = None
    for e in range(n_e):
        part = parts_ref[e].astype(F32)
        for r in range(1, n_r):
            part = part + parts_ref[r * n_e + e].astype(F32)
        part = part * share_ref[:, e:e + 1]
        total = part if total is None else total + part
    c = lax.axis_index("ctx")
    col = (iota(total.shape, 0) // n_b) * 128 + iota(total.shape, 1)
    mine = (col >= c * width) & (col < (c + 1) * width)
    total = total + jnp.where(mine, hid_ref[...].astype(F32), 0.0)
    for i in range(n_c):
        h, off = divmod(i * width, 128)
        n = min(width, 128 - off)
        out_ref[i, :, 0:n] = total[h * n_b:(h + 1) * n_b, off:off + n]
        if n < width:
            out_ref[i, :, n:width] = total[(h + 1) * n_b:(h + 2) * n_b, 0:width - n]


def sum_kernel(parts_ref, out_ref):
    total = jnp.sum(parts_ref[...], axis=0)
    out_ref[...] = total[:, 0:out_ref.shape[1]].astype(BF16)


def body(
    queries,
    cache_keys,
    cache_values,
    residual,
    lengths,
    expert_ids,
    router,
    gate_weight,
    up_weight,
    down_weight,
):
    n_b, n_h, size = queries.shape
    here = cache_keys.shape[2]
    n_c, n_r, n_e = (lax.axis_size(a) for a in ("ctx", "rows", "expert"))
    rows = n_b * n_h
    struct = jax.ShapeDtypeStruct
    q = queries.transpose(1, 0, 2).reshape(rows, size)
    keys = cache_keys.reshape(n_b, here, size)
    values = cache_values.reshape(n_b, here, size)

    def swap(x, axes):
        return lax.all_to_all(x, axes, split_axis=0, concat_axis=0, tiled=True)

    dims = size * n_b // n_c
    sent = call(
        functools.partial(score_kernel, n_h), struct((n_c, dims + 16, here), BF16),
        keys, q, lengths, residual, values, specs=[HBM] * 5, out_spec=HBM,
        scratch=[
            pltpu.VMEM((n_c, dims + 16, here), BF16), pltpu.VMEM(keys.shape, BF16), pltpu.VMEM(q.shape, BF16),
            pltpu.SMEM((n_b,), jnp.int32), pltpu.VMEM(residual.shape, BF16), pltpu.VMEM(values.shape, BF16),
            pltpu.SemaphoreType.DMA((5,)), pltpu.SemaphoreType.DMA((n_b,)),
        ],
        limit=60 << 20,
    )
    got = swap(sent, "ctx")
    sent = call(
        functools.partial(attend_kernel, n_h, n_c // n_b), struct((n_c, 8, size), BF16), got, specs=[VMEM],
    )
    got = swap(sent, "ctx")
    hidden, sent = call(
        hidden_kernel, (struct((rows, size), BF16), struct((n_r * n_e, rows, size), BF16)), got, specs=[VMEM],
    )
    got = swap(sent, ("rows", "expert")).reshape(n_r, n_e * rows, size)
    sent, share = call(
        expert_kernel, (struct((n_r, n_e, rows, size), BF16), struct((rows, n_e), F32)),
        expert_ids.T, got, router.T, gate_weight[0], up_weight[0], down_weight[0],
        specs=[SMEM, VMEM, VMEM, VMEM, VMEM, VMEM],
        scratch=[
            pltpu.VMEM((n_r, n_e, rows, size), F32)],
    )
    got = swap(sent.reshape(n_r * n_e, rows, size), ("rows", "expert"))
    width = n_h * size // n_c
    sent = call(
        functools.partial(split_kernel, width), struct((n_c, n_b, 128), F32),
        got, share, hidden, specs=[VMEM, VMEM, VMEM],
    )
    return call(sum_kernel, struct((n_b, width), BF16), swap(sent, "ctx"), specs=[VMEM])


def solution(mesh):
    placed = (
        P("expert", "rows", None),
        P("expert", "rows", "ctx", None),
        P("expert", "rows", "ctx", None),
        P("expert", "rows"),
        P("expert"),
        P("expert", None),
        P(),
        P("expert", None, ("rows", "ctx")),
        P("expert", None, ("rows", "ctx")),
        P("expert", ("rows", "ctx"), None),
    )
    return jax.shard_map(
        body, mesh=mesh, in_specs=placed, out_specs=P("expert", ("rows", "ctx")), check_vma=False
    )
```

time: 1200 us -> 98.2 us (0.08)
  waiting for transfers between devices: 685 us -> 0 us
  blocking collectives: 329 us -> 91.7 us
  starting transfers between devices: 130 us -> 0 us
  local copies, waits for them, and re-layouts: 19 us -> 0.02 us
  other arithmetic: 14.6 us -> 0 us
  between operations: 13.4 us -> 0.06 us
    unnamed x2 -> x0, waiting for transfers between devices: 677 us -> none
    psum x13 -> x0, blocking collectives: 289 us -> none  [the longest x12 250 us: one_round(): total_now = lax.psum(local_mass(scaled, usable, middle_now), 'ctx')]
    all_to_all x2 -> x0, starting transfers between devices: 130 us -> none  [the longest x1 114 us: body(): lax.all_to_all(outgoing, 'expert', split_axis=0, concat_axis=0, tiled=True)]
    all_to_all x0 -> x5, blocking collectives: none -> 91.7 us  [swap(): return lax.all_to_all(x, axes, split_axis=0, concat_axis=0, tiled=True)]
    pmax x1 -> x0, blocking collectives: 30.5 us -> none  [body(): top_score = lax.pmax(local_top, 'ctx')]
  transfers between devices with their start and end apart: 3 -> 0, of which waited for: 3 -> 0; matrix products, arithmetic and copies ran while one was open for 0% -> 0% of each run, Pallas kernels for 0% -> 0%
where the time goes in v1:
time: 98.2 us; the launch traced here: 97.9 us
  blocking collectives  91.7 us (93%)
  Pallas kernels  6.13 us (6%)
    all_to_all x5, blocking collectives, swap(): return lax.all_to_all(x, axes, split_axis=0, concat_axis=0, tiled=True)  91.7 us
    pallas_call x6, Pallas kernels, call(): pl.pallas_call(kernel, out_shape=outs, in_specs=specs, out_specs=jax.tree...  6.13 us

profile of v1, /device:TPU:1, one launch (start us, length us, event | category | flops | bytes accessed | tf_op | source)
XLA Modules:
  0.0 97.9 jit_solution(7159031888363025711)
XLA Ops:
  0.0 2.3 %shard_map.100 = bf16[16,48,128]{2,1,0:T(8,128)(2,1)} custom-call(bf16[4,128,128]{2,1,0:T(8,128)(2,1)} %bitcast.19, bf16[24,128]{1,0:T(8,128)(2,1)} %bitcast.21, s32[4]{0:T(128)} %len_hbm.1, bf16[4,768]{1,0:T(4,128)(2,1)} %res_hbm.1, bf16[4,128,128]{2,1,0:T(8,128)(2,1)} %bitcast.20), custom_call_target="tpu_custom_call" | custom-call | flops 68719476736 | bytes 268435456 | tf_op jit(solution)/shard_map/pallas_call | solution.py:22
  2.3 28.3 %all_to_all.25.got_ref = bf16[16,48,128]{2,1,0:T(8,128)(2,1)S(1)} all-to-all(bf16[16,48,128]{2,1,0:T(8,128)(2,1)} %shard_map.100), channel_id=1, replica_groups=mesh['rows'=4,'ctx'=16,'expert'=8] {'ctx'}, dimensions={0} | all-to-all | bytes 393216 | tf_op jit(solution)/shard_map/all_to_all | solution.py:265
  30.6 0.9 shard_map.101
  31.5 20.1 %all_to_all.26.got_ref = bf16[16,8,128]{2,1,0:T(8,128)(2,1)S(1)} all-to-all(bf16[16,8,128]{2,1,0:T(8,128)(2,1)S(1)} %shard_map.101), channel_id=1, replica_groups=mesh['rows'=4,'ctx'=16,'expert'=8] {'ctx'}, dimensions={0} | all-to-all | bytes 65536 | tf_op jit(solution)/shard_map/all_to_all | solution.py:265
  51.6 0.0 copy-start
  51.6 0.0 copy-start.1
  51.6 0.0 copy-start.2
  51.6 0.0 copy-start.3
  51.6 0.0 copy-start.4
  51.7 0.1 shard_map.102
  51.8 17.4 %all_to_all.27 = bf16[32,24,128]{2,1,0:T(8,128)(2,1)S(1)} all-to-all(bf16[32,24,128]{2,1,0:T(8,128)(2,1)S(1)} %get-tuple-element.9), channel_id=1, replica_groups=mesh['rows'=4,'ctx'=16,'expert'=8] {'rows','expert'}, dimensions={0} | all-to-all | bytes 393216 | tf_op jit(solution)/shard_map/all_to_all | solution.py:265
  69.2 0.0 copy-done
  69.2 0.0 copy-done.1
  69.2 0.0 copy-done.2
  69.2 0.0 copy-done.3
  69.3 0.0 copy-done.4
  69.3 2.0 %shard_map.103 = (bf16[4,8,24,128]{3,2,1,0:T(8,128)(2,1)S(1)}, f32[24,8]{1,0:T(8,128)S(1)}) custom-call(s32[2,4]{1,0:T(2,128)S(1)} %bitcast.18, bf16[4,192,128]{2,1,0:T(8,128)(2,1)S(1)} %bitcast.12, f32[8,3072]{1,0:T(8,128)S(1)} %bitcast.17, bf16[3072,256]{1,0:T(8,128)(2,1)S(1)} %bitcast.14, bf16[3072,256]{1,0:T(8,128)(2,1)S(1)} %bitcast.15, ...), custom_call_target="tpu_custom_call" | custom-call | flops 68719476736 | bytes 268435456 | tf_op jit(solution)/shard_map/pallas_call | solution.py:22
  71.3 11.9 %all_to_all.28.parts_ref = bf16[32,24,128]{2,1,0:T(8,128)(2,1)S(1)} all-to-all(bf16[32,24,128]{2,1,0:T(8,128)(2,1)S(1)} %bitcast.13), channel_id=1, replica_groups=mesh['rows'=4,'ctx'=16,'expert'=8] {'rows','expert'}, dimensions={0} | all-to-all | bytes 393216 | tf_op jit(solution)/shard_map/all_to_all | solution.py:265
  83.1 0.2 shard_map.104
  83.3 14.0 %all_to_all.29.parts_ref = f32[16,4,128]{2,1,0:T(4,128)S(1)} all-to-all(f32[16,4,128]{2,1,0:T(4,128)S(1)} %shard_map.104), channel_id=1, replica_groups=mesh['rows'=4,'ctx'=16,'expert'=8] {'ctx'}, dimensions={0} | all-to-all | bytes 65536 | tf_op jit(solution)/shard_map/all_to_all | solution.py:265
  97.3 0.6 shard_map.105
Async XLA Ops:
  51.6 17.6 %copy-start = (bf16[1,3072,256]{2,1,0:T(8,128)(2,1)S(1)}, bf16[1,3072,256]{2,1,0:T(8,128)(2,1)}, u32[]{:S(2)}) copy-start(bf16[1,3072,256]{2,1,0:T(8,128)(2,1)} %param.17) | copy-start | bytes 4718596
  51.6 17.6 %copy-start.1 = (bf16[1,3072,256]{2,1,0:T(8,128)(2,1)S(1)}, bf16[1,3072,256]{2,1,0:T(8,128)(2,1)}, u32[]{:S(2)}) copy-start(bf16[1,3072,256]{2,1,0:T(8,128)(2,1)} %param.18) | copy-start | bytes 4718596
  51.6 17.6 %copy-start.2 = (bf16[1,256,3072]{2,1,0:T(8,128)(2,1)S(1)}, bf16[1,256,3072]{2,1,0:T(8,128)(2,1)}, u32[]{:S(2)}) copy-start(bf16[1,256,3072]{2,1,0:T(8,128)(2,1)} %param.19) | copy-start | bytes 4718596
  51.6 17.6 %copy-start.3 = (f32[3072,8]{0,1:T(8,128)S(1)}, f32[3072,8]{0,1:T(8,128)}, u32[]{:S(2)}) copy-start(f32[3072,8]{0,1:T(8,128)} %param.16) | copy-start | bytes 294916
  51.6 17.6 %copy-start.4 = (s32[4,2]{0,1:T(2,128)S(1)}, s32[4,2]{0,1:T(2,128)}, u32[]{:S(2)}) copy-start(s32[4,2]{0,1:T(2,128)} %param.15) | copy-start | bytes 100

commit v2 on v1

--- a/solution.py
+++ b/solution.py
@@ -61,17 +61,17 @@
     place = c * here + iota((8, here), 1)
     eye = one_hot(iota((size, size), 0) == iota((size, size), 1))
     diagonal = iota((8, here), 0) == iota((8, here), 1)
-    head = iota((8, heads * n_b), 0)
+    at, src = iota((8 * n_b, heads * n_b), 0), iota((8 * n_b, heads * n_b), 1)
+    pick = one_hot(src == at % 8 * n_b + at // 8)
     for copy in copies[:4]:
         copy.wait()
-    q = q_ref[...]
+    q = jnp.dot(pick, q_ref[...], preferred_element_type=F32)
     res = res_ref[...].astype(F32)
     odd = lax.rem(c, 2) == 1
     half = heads // 2
     tails = []
     for b in range(n_b):
-        pick = one_hot((iota(head.shape, 1) == head * n_b + b) & (head < heads))
-        q_b = jnp.dot(pick, q, preferred_element_type=F32).astype(BF16)
+        q_b = q[8 * b:8 * b + 8].astype(BF16)
         scaled = lax.dot_general(q_b, k_ref[b], NT, preferred_element_type=F32) * (0.5 / math.sqrt(size))
         valid = place < len_ref[b]
         top = jnp.max(jnp.where(valid, scaled, NEG), axis=-1, keepdims=True)
@@ -137,11 +137,15 @@
     weights = jnp.concatenate([weights[i] for i in range(n_c)], axis=1).astype(BF16)
     values = jnp.concatenate([got_ref[i, 0:dims] for i in range(n_c)], axis=1)
     attended = lax.dot_general(weights, values, NT, preferred_element_type=F32) / total
-    attended = jnp.concatenate([attended] * split, axis=1)
-    res = [parts[i, 2 * heads + 1:] for i in range(2)]
-    res = jnp.concatenate(res + [jnp.zeros((8 - heads, here), F32)], axis=0)
-    mine = (iota(res.shape, 1) // dims == j) & (iota(res.shape, 0) < heads)
-    piece = jnp.where(mine, res + attended, 0.0).astype(BF16)
+    res = jnp.concatenate([parts[i, 2 * heads + 1:] for i in range(2)] + [jnp.zeros((8 - heads, here), F32)], axis=0)
+    mine = res[:, 0:dims]
+    for k in range(1, split):
+        mine = jnp.where(j == k, res[:, k * dims:(k + 1) * dims], mine)
+    hidden = mine + attended
+    flat = [hidden[h:h + 1] for h in range(heads)]
+    flat += [jnp.zeros((1, dims), F32)] * (-heads % split)
+    lines = [jnp.concatenate(flat[h:h + split], axis=1) for h in range(0, len(flat), split)]
+    piece = jnp.concatenate(lines, axis=0).astype(BF16)
     for i in range(n_c):
         out_ref[i] = piece
 
@@ -151,24 +155,26 @@
     rows, size = hid_ref.shape
     n_b = 4
     split = n_c // n_b
+    dims = size // split
+    at, src = iota((n_c, n_c), 0), iota((n_c, n_c), 1)
+    pick = one_hot(src == (at % n_b) * split + at // n_b)
     got = got_ref[...].astype(F32)
-    whole = []
-    for b in range(n_b):
-        row = got[b * split]
-        for j in range(1, split):
-            row = row + got[b * split + j]
-        whole.append(row)
-    whole = jnp.concatenate(whole, axis=0).astype(BF16)
-    at, src = iota((rows, 8 * n_b), 0), iota((rows, 8 * n_b), 1)
-    pick = one_hot(src == (at % n_b) * 8 + at // n_b)
-    hidden = jnp.dot(pick, whole, preferred_element_type=F32).astype(BF16)
+    moved = [
+        jnp.dot(pick, got[:, k].astype(BF16), preferred_element_type=F32) for k in range(got_ref.shape[1])
+    ]
+    pieces = []
+    for h in range(rows // n_b):
+        lanes = slice(h % split * dims, (h % split + 1) * dims)
+        from_j = [moved[h // split][j * n_b:(j + 1) * n_b, lanes] for j in range(split)]
+        pieces.append(jnp.concatenate(from_j, axis=1))
+    hidden = jnp.concatenate(pieces, axis=0).astype(BF16)
     hid_ref[...] = hidden
     for i in range(out_ref.shape[0]):
         out_ref[i] = hidden
 
 
 def expert_kernel(
-    ids_ref, g_ref, router_ref, gate_ref, up_ref, down_ref, out_ref, share_ref, wide_ref
+    ids_ref, g_ref, router_ref, gate_ref, up_ref, down_ref, out_ref, share_ref, logit_ref
 ):
     n_r, n_e, block, _ = out_ref.shape
     n_b = 4
@@ -178,8 +184,10 @@
     at, src = iota((heads * rows, n_e * block), 0), iota((heads * rows, n_e * block), 1)
     inner = at % rows
     pick = one_hot(src == (inner // n_b) * block + (at // rows) * n_b + inner % n_b)
-    own = one_hot(iota((block, rows), 1) == lax.axis_index("expert") * n_b + iota((block, rows), 0) % n_b)
-    routers = parts_of(router_ref[...], 3)
+    at, src = iota((n_e * block, heads * rows), 0), iota((n_e * block, heads * rows), 1)
+    inner = at % block
+    back = one_hot(src == inner // n_b * rows + at // block * n_b + inner % n_b)
+    router = jnp.concatenate([part.astype(F32) for part in parts_of(router_ref[...], 3)], axis=0).astype(BF16)
     gate = up = logits = None
     for r in range(n_r):
         moved = jnp.dot(pick, g_ref[r], preferred_element_type=F32).astype(BF16)
@@ -187,24 +195,24 @@
         cols = slice(r * width, (r + 1) * width)
         g = jnp.dot(x, gate_ref[cols], preferred_element_type=F32)
         u = jnp.dot(x, up_ref[cols], preferred_element_type=F32)
-        x_own = jnp.dot(own, x, preferred_element_type=F32).astype(BF16)
-        hi, mid, low = [lax.dot_general(x_own, m[:, cols], NT, preferred_element_type=F32) for m in routers]
-        l = (low + mid) + hi
+        l = lax.dot_general(x, router[:, cols], NT, preferred_element_type=F32)
         gate, up, logits = (g, u, l) if r == 0 else (gate + g, up + u, logits + l)
     act = ((gate / (1.0 + jnp.exp(-gate))) * up).astype(BF16)
     for r in range(n_r):
-        o = jnp.dot(act, down_ref[:, r * width:(r + 1) * width], preferred_element_type=F32)
-        for h in range(heads):
-            piece = o[:, h * 128:(h + 1) * 128]
-            for e in range(n_e):
-                wide_ref[r, e, h * n_b:(h + 1) * n_b, :] = piece[e * n_b:(e + 1) * n_b]
-    out_ref[...] = wide_ref[...].astype(BF16)
+        o = jnp.dot(act, down_ref[:, r * width:(r + 1) * width], preferred_element_type=F32).astype(BF16)
+        o = jnp.concatenate([o[:, h * 128:(h + 1) * 128] for h in range(heads)], axis=0)
+        o = jnp.dot(back, o, preferred_element_type=F32)
+        for e in range(n_e):
+            out_ref[r, e] = o[e * block:(e + 1) * block].astype(BF16)
+    logit_ref[...] = (logits[:, 2 * n_e:3 * n_e] + logits[:, n_e:2 * n_e]) + logits[:, 0:n_e]
+    logits = logit_ref[pl.ds(lax.axis_index("expert") * n_b, n_b), :]
+    logits = jnp.concatenate([logits] * heads, axis=0)
     which = iota(logits.shape, 1)
     owner = iota(logits.shape, 0) % n_b
     first = second = jnp.zeros(logits.shape, jnp.int32)
     for b in range(n_b):
-        first = jnp.where(owner == b, ids_ref[0, b], first)
-        second = jnp.where(owner == b, ids_ref[1, b], second)
+        first = jnp.where(owner == b, ids_ref[0:1, b:b + 1], first)
+        second = jnp.where(owner == b, ids_ref[1:2, b:b + 1], second)
     l0 = jnp.sum(jnp.where(which == first, logits, 0.0), axis=-1, keepdims=True)
     l1 = jnp.sum(jnp.where(which == second, logits, 0.0), axis=-1, keepdims=True)
     s0 = 1.0 / (1.0 + jnp.exp(l1 - l0))
@@ -213,7 +221,7 @@
 
 
 def split_kernel(width, parts_ref, share_ref, hid_ref, out_ref):
-    n_c, n_b, _ = out_ref.shape
+    n_c, n_b = out_ref.shape[0], 4
     n_e = share_ref.shape[1]
     n_r = parts_ref.shape[0] // n_e
     total = None
@@ -277,7 +285,7 @@
     )
     got = swap(sent, "ctx")
     sent = call(
-        functools.partial(attend_kernel, n_h, n_c // n_b), struct((n_c, 8, size), BF16), got, specs=[VMEM],
+        functools.partial(attend_kernel, n_h, n_c // n_b), struct((n_c, -(-n_h * n_b // n_c), size), BF16), got, specs=[VMEM],
     )
     got = swap(sent, "ctx")
     hidden, sent = call(
@@ -287,9 +295,9 @@
     sent, share = call(
         expert_kernel, (struct((n_r, n_e, rows, size), BF16), struct((rows, n_e), F32)),
         expert_ids.T, got, router.T, gate_weight[0], up_weight[0], down_weight[0],
-        specs=[SMEM, VMEM, VMEM, VMEM, VMEM, VMEM],
+        specs=[VMEM] * 6,
         scratch=[
-            pltpu.VMEM((n_r, n_e, rows, size), F32)],
+            pltpu.VMEM((n_e * n_b, n_e), F32)],
     )
     got = swap(sent.reshape(n_r * n_e, rows, size), ("rows", "expert"))
     width = n_h * size // n_c

time: 98.2 us -> 98.1 us (level)
  no operation moved by 1% of the time
where the time goes in v2:
time: 98.1 us; the launch traced here: 97.7 us
  blocking collectives  91.5 us (93%)
  Pallas kernels  6.09 us (6%)
    all_to_all x5, blocking collectives, swap(): return lax.all_to_all(x, axes, split_axis=0, concat_axis=0, tiled=True)  91.5 us
    pallas_call x6, Pallas kernels, call(): pl.pallas_call(kernel, out_shape=outs, in_specs=specs, out_specs=jax.tree...  6.09 us

profile of v2, /device:TPU:1, one launch (start us, length us, event | category | flops | bytes accessed | tf_op | source)
XLA Modules:
  0.0 97.7 jit_solution(18227313769717151987)
XLA Ops:
  0.0 2.2 %shard_map.100 = bf16[16,48,128]{2,1,0:T(8,128)(2,1)} custom-call(bf16[4,128,128]{2,1,0:T(8,128)(2,1)} %bitcast.19, bf16[24,128]{1,0:T(8,128)(2,1)} %bitcast.21, s32[4]{0:T(128)} %len_hbm.1, bf16[4,768]{1,0:T(4,128)(2,1)} %res_hbm.1, bf16[4,128,128]{2,1,0:T(8,128)(2,1)} %bitcast.20), custom_call_target="tpu_custom_call" | custom-call | flops 68719476736 | bytes 268435456 | tf_op jit(solution)/shard_map/pallas_call | solution.py:22
  2.2 28.3 %all_to_all.25.got_ref = bf16[16,48,128]{2,1,0:T(8,128)(2,1)S(1)} all-to-all(bf16[16,48,128]{2,1,0:T(8,128)(2,1)} %shard_map.100), channel_id=1, replica_groups=mesh['rows'=4,'ctx'=16,'expert'=8] {'ctx'}, dimensions={0} | all-to-all | bytes 393216 | tf_op jit(solution)/shard_map/all_to_all | solution.py:273
  30.5 1.0 %shard_map.101 = bf16[16,2,128]{2,1,0:T(2,128)(2,1)S(1)} custom-call(bf16[16,48,128]{2,1,0:T(8,128)(2,1)S(1)} %all_to_all.25.got_ref), custom_call_target="tpu_custom_call" | custom-call | flops 68719476736 | bytes 268435456 | tf_op jit(solution)/shard_map/pallas_call | solution.py:22
  31.5 19.9 %all_to_all.26.got_ref = bf16[16,2,128]{2,1,0:T(2,128)(2,1)S(1)} all-to-all(bf16[16,2,128]{2,1,0:T(2,128)(2,1)S(1)} %shard_map.101), channel_id=1, replica_groups=mesh['rows'=4,'ctx'=16,'expert'=8] {'ctx'}, dimensions={0} | all-to-all | bytes 16384 | tf_op jit(solution)/shard_map/all_to_all | solution.py:273
  51.4 0.0 copy-start
  51.4 0.0 copy-start.1
  51.4 0.0 copy-start.2
  51.5 0.0 copy-start.3
  51.5 0.0 copy-start.4
  51.5 0.2 shard_map.102
  51.7 17.5 %all_to_all.27 = bf16[32,24,128]{2,1,0:T(8,128)(2,1)S(1)} all-to-all(bf16[32,24,128]{2,1,0:T(8,128)(2,1)S(1)} %get-tuple-element.9), channel_id=1, replica_groups=mesh['rows'=4,'ctx'=16,'expert'=8] {'rows','expert'}, dimensions={0} | all-to-all | bytes 393216 | tf_op jit(solution)/shard_map/all_to_all | solution.py:273
  69.2 0.0 copy-done
  69.2 0.0 copy-done.1
  69.2 0.0 copy-done.2
  69.2 0.0 copy-done.3
  69.2 0.0 copy-done.4
  69.2 1.9 %shard_map.103 = (bf16[4,8,24,128]{3,2,1,0:T(8,128)(2,1)S(1)}, f32[24,8]{1,0:T(8,128)S(1)}) custom-call(s32[2,4]{1,0:T(2,128)S(1)} %bitcast.18, bf16[4,192,128]{2,1,0:T(8,128)(2,1)S(1)} %bitcast.12, f32[8,3072]{1,0:T(8,128)S(1)} %bitcast.17, bf16[3072,256]{1,0:T(8,128)(2,1)S(1)} %bitcast.14, bf16[3072,256]{1,0:T(8,128)(2,1)S(1)} %bitcast.15, ...), custom_call_target="tpu_custom_call" | custom-call | flops 68719476736 | bytes 268435456 | tf_op jit(solution)/shard_map/pallas_call | solution.py:22
  71.1 11.9 %all_to_all.28.parts_ref = bf16[32,24,128]{2,1,0:T(8,128)(2,1)S(1)} all-to-all(bf16[32,24,128]{2,1,0:T(8,128)(2,1)S(1)} %bitcast.13), channel_id=1, replica_groups=mesh['rows'=4,'ctx'=16,'expert'=8] {'rows','expert'}, dimensions={0} | all-to-all | bytes 393216 | tf_op jit(solution)/shard_map/all_to_all | solution.py:273
  83.0 0.2 shard_map.104
  83.2 14.0 %all_to_all.29.parts_ref = f32[16,4,128]{2,1,0:T(4,128)S(1)} all-to-all(f32[16,4,128]{2,1,0:T(4,128)S(1)} %shard_map.104), channel_id=1, replica_groups=mesh['rows'=4,'ctx'=16,'expert'=8] {'ctx'}, dimensions={0} | all-to-all | bytes 65536 | tf_op jit(solution)/shard_map/all_to_all | solution.py:273
  97.1 0.6 shard_map.105
Async XLA Ops:
  51.4 17.7 %copy-start = (bf16[1,3072,256]{2,1,0:T(8,128)(2,1)S(1)}, bf16[1,3072,256]{2,1,0:T(8,128)(2,1)}, u32[]{:S(2)}) copy-start(bf16[1,3072,256]{2,1,0:T(8,128)(2,1)} %param.17) | copy-start | bytes 4718596
  51.4 17.7 %copy-start.1 = (bf16[1,3072,256]{2,1,0:T(8,128)(2,1)S(1)}, bf16[1,3072,256]{2,1,0:T(8,128)(2,1)}, u32[]{:S(2)}) copy-start(bf16[1,3072,256]{2,1,0:T(8,128)(2,1)} %param.18) | copy-start | bytes 4718596
  51.4 17.7 %copy-start.2 = (bf16[1,256,3072]{2,1,0:T(8,128)(2,1)S(1)}, bf16[1,256,3072]{2,1,0:T(8,128)(2,1)}, u32[]{:S(2)}) copy-start(bf16[1,256,3072]{2,1,0:T(8,128)(2,1)} %param.19) | copy-start | bytes 4718596
  51.5 17.7 %copy-start.3 = (f32[3072,8]{0,1:T(8,128)S(1)}, f32[3072,8]{0,1:T(8,128)}, u32[]{:S(2)}) copy-start(f32[3072,8]{0,1:T(8,128)} %param.16) | copy-start | bytes 294916
  51.5 17.7 %copy-start.4 = (s32[4,2]{0,1:T(2,128)S(1)}, s32[4,2]{0,1:T(2,128)}, u32[]{:S(2)}) copy-start(s32[4,2]{0,1:T(2,128)} %param.15) | copy-start | bytes 100

commit v3 on v2

--- a/solution.py
+++ b/solution.py
@@ -14,6 +14,9 @@
 F32 = jnp.float32
 BF16 = jnp.bfloat16
 NEG = -1e30
+FAR = 1.25
+SCALE = 143.0
+SHIFT = 80.0
 HBM = pl.BlockSpec(memory_space=pltpu.HBM)
 NT = (((1,), (1,)), ((), ()))
 
@@ -48,9 +51,9 @@
 
 
 def score_kernel(
-    heads, k_hbm, q_hbm, len_hbm, res_hbm, v_hbm, out_hbm, out_ref, k_ref, q_ref, len_ref, res_ref, v_ref, sems, out_sems
+    heads, k_hbm, q_hbm, len_hbm, v_hbm, out_hbm, out_ref, k_ref, q_ref, len_ref, v_ref, sems, out_sems
 ):
-    pairs = ((k_hbm, k_ref), (q_hbm, q_ref), (len_hbm, len_ref), (res_hbm, res_ref), (v_hbm, v_ref))
+    pairs = ((k_hbm, k_ref), (q_hbm, q_ref), (len_hbm, len_ref), (v_hbm, v_ref))
     copies = [pltpu.make_async_copy(src, dst, sems.at[i]) for i, (src, dst) in enumerate(pairs)]
     for copy in copies:
         copy.start()
@@ -63,26 +66,27 @@
     diagonal = iota((8, here), 0) == iota((8, here), 1)
     at, src = iota((8 * n_b, heads * n_b), 0), iota((8 * n_b, heads * n_b), 1)
     pick = one_hot(src == at % 8 * n_b + at // 8)
-    for copy in copies[:4]:
+    for copy in copies[:3]:
         copy.wait()
     q = jnp.dot(pick, q_ref[...], preferred_element_type=F32)
-    res = res_ref[...].astype(F32)
-    odd = lax.rem(c, 2) == 1
-    half = heads // 2
     tails = []
     for b in range(n_b):
         q_b = q[8 * b:8 * b + 8].astype(BF16)
         scaled = lax.dot_general(q_b, k_ref[b], NT, preferred_element_type=F32) * (0.5 / math.sqrt(size))
         valid = place < len_ref[b]
         top = jnp.max(jnp.where(valid, scaled, NEG), axis=-1, keepdims=True)
-        top = jnp.where(top > 0.5 * NEG, top.astype(BF16).astype(F32), 0.0)
-        rows = [part.astype(F32)[0:heads] for part in parts_of(jnp.where(valid, scaled - top, NEG), 2)]
-        rows.append(jnp.sum(jnp.where(diagonal, top, 0.0), axis=0, keepdims=True))
-        for k in range(half):
-            even_part, odd_part = (res[b:b + 1, h * size:(h + 1) * size] for h in (k, half + k))
-            rows.append(jnp.where(odd, odd_part, even_part))
+        coarse = top.astype(BF16).astype(F32)
+        fine = top - coarse
+        fine = (fine + jnp.abs(fine) * (1.0 / 128.0)).astype(BF16).astype(F32)
+        below = jnp.where(valid, jnp.minimum((coarse + fine) - scaled, FAR), FAR)
+        coded = jnp.exp(SCALE * jnp.sqrt(jnp.maximum(below, 0.0)) - SHIFT)
+        count = jnp.sum(jnp.where(valid, 1.0, 0.0)[0:1], axis=-1, keepdims=True)
+        tops = [jnp.sum(jnp.where(diagonal, part, 0.0), axis=0, keepdims=True) for part in (coarse, fine)]
+        lane = iota((1, here), 1)
+        tops[0] = jnp.where(lane < 8, tops[0], count)
+        rows = [coded[0:heads]] + tops
         tails.append(jnp.concatenate(rows, axis=0))
-    copies[4].wait()
+    copies[3].wait()
     out_copies = []
     for b in range(n_b):
         turned = lax.dot_general(eye, v_ref[b], NT, preferred_element_type=F32)
@@ -96,18 +100,17 @@
         copy.wait()
 
 
-def attend_kernel(heads, split, got_ref, out_ref):
+def attend_kernel(heads, split, got_ref, res_ref, out_ref):
     n_c, rows, here = got_ref.shape
-    dims = rows - 16
-    j = lax.axis_index("ctx") % split
+    dims = rows - 8
+    b, j = lax.axis_index("ctx") // split, lax.axis_index("ctx") % split
     parts = got_ref[:, dims:].astype(F32)
     diagonal = iota((n_c, 8, here), 1) == iota((n_c, 8, here), 2)
-    tops = jnp.sum(jnp.where(diagonal, parts[:, 2 * heads:2 * heads + 1], 0.0), axis=-1, keepdims=True)
-    blank = jnp.full((8 - heads, here), NEG, F32)
-    scores = [jnp.concatenate([parts[i, 0:heads] + parts[i, heads:2 * heads], blank], axis=0) for i in range(n_c)]
-    scores = jnp.stack(scores) + tops
-    count = jnp.sum(jnp.sum(jnp.where(scores > 0.5 * NEG, 1.0, 0.0), axis=0), axis=-1, keepdims=True)
-    count = jnp.maximum(count, 1.0)
+    tops = parts[:, heads:heads + 1] + parts[:, heads + 1:heads + 2]
+    tops = jnp.sum(jnp.where(diagonal, tops, 0.0), axis=-1, keepdims=True)
+    root = (jnp.log(parts) + SHIFT) * (1.0 / SCALE)
+    scores = jnp.where(iota(root.shape, 1) < heads, tops - root * root, NEG)
+    count = jnp.sum(parts[:, heads:heads + 1, 8:9], axis=0)
     top = jnp.max(jnp.max(scores, axis=0), axis=-1, keepdims=True)
     low = top - 1.0
     interval = (top - 1.0 / jnp.sqrt(count)) - low
@@ -137,7 +140,10 @@
     weights = jnp.concatenate([weights[i] for i in range(n_c)], axis=1).astype(BF16)
     values = jnp.concatenate([got_ref[i, 0:dims] for i in range(n_c)], axis=1)
     attended = lax.dot_general(weights, values, NT, preferred_element_type=F32) / total
-    res = jnp.concatenate([parts[i, 2 * heads + 1:] for i in range(2)] + [jnp.zeros((8 - heads, here), F32)], axis=0)
+    res = res_ref[...].astype(F32)
+    res = jnp.sum(jnp.where(iota(res.shape, 0) == b, res, 0.0), axis=0, keepdims=True)
+    res = [res[:, h * here:(h + 1) * here] for h in range(heads)]
+    res = jnp.concatenate(res + [jnp.zeros((8 - heads, here), F32)], axis=0)
     mine = res[:, 0:dims]
     for k in range(1, split):
         mine = jnp.where(j == k, res[:, k * dims:(k + 1) * dims], mine)
@@ -238,14 +244,18 @@
     for i in range(n_c):
         h, off = divmod(i * width, 128)
         n = min(width, 128 - off)
-        out_ref[i, :, 0:n] = total[h * n_b:(h + 1) * n_b, off:off + n]
+        piece = total[h * n_b:(h + 1) * n_b, off:off + n]
         if n < width:
-            out_ref[i, :, n:width] = total[(h + 1) * n_b:(h + 2) * n_b, 0:width - n]
+            piece = jnp.concatenate([piece, total[(h + 1) * n_b:(h + 2) * n_b, 0:width - n]], axis=1)
+        for b in range(n_b):
+            out_ref[i, b // 2:b // 2 + 1, b % 2 * width:(b % 2 + 1) * width] = piece[b:b + 1]
 
 
 def sum_kernel(parts_ref, out_ref):
     total = jnp.sum(parts_ref[...], axis=0)
-    out_ref[...] = total[:, 0:out_ref.shape[1]].astype(BF16)
+    n_b, width = out_ref.shape
+    rows = [total[b // 2:b // 2 + 1, b % 2 * width:(b % 2 + 1) * width] for b in range(n_b)]
+    out_ref[...] = jnp.concatenate(rows, axis=0).astype(BF16)
 
 
 def body(
@@ -274,18 +284,19 @@
 
     dims = size * n_b // n_c
     sent = call(
-        functools.partial(score_kernel, n_h), struct((n_c, dims + 16, here), BF16),
-        keys, q, lengths, residual, values, specs=[HBM] * 5, out_spec=HBM,
+        functools.partial(score_kernel, n_h), struct((n_c, dims + 8, here), BF16),
+        keys, q, lengths, values, specs=[HBM] * 4, out_spec=HBM,
         scratch=[
-            pltpu.VMEM((n_c, dims + 16, here), BF16), pltpu.VMEM(keys.shape, BF16), pltpu.VMEM(q.shape, BF16),
-            pltpu.SMEM((n_b,), jnp.int32), pltpu.VMEM(residual.shape, BF16), pltpu.VMEM(values.shape, BF16),
-            pltpu.SemaphoreType.DMA((5,)), pltpu.SemaphoreType.DMA((n_b,)),
+            pltpu.VMEM((n_c, dims + 8, here), BF16), pltpu.VMEM(keys.shape, BF16), pltpu.VMEM(q.shape, BF16),
+            pltpu.SMEM((n_b,), jnp.int32), pltpu.VMEM(values.shape, BF16),
+            pltpu.SemaphoreType.DMA((4,)), pltpu.SemaphoreType.DMA((n_b,)),
         ],
         limit=60 << 20,
     )
     got = swap(sent, "ctx")
     sent = call(
-        functools.partial(attend_kernel, n_h, n_c // n_b), struct((n_c, -(-n_h * n_b // n_c), size), BF16), got, specs=[VMEM],
+        functools.partial(attend_kernel, n_h, n_c // n_b), struct((n_c, -(-n_h * n_b // n_c), size), BF16), got, residual,
+        specs=[VMEM, VMEM],
     )
     got = swap(sent, "ctx")
     hidden, sent = call(
@@ -302,7 +313,7 @@
     got = swap(sent.reshape(n_r * n_e, rows, size), ("rows", "expert"))
     width = n_h * size // n_c
     sent = call(
-        functools.partial(split_kernel, width), struct((n_c, n_b, 128), F32),
+        functools.partial(split_kernel, width), struct((n_c, n_b // 2, 2 * width), F32),
         got, share, hidden, specs=[VMEM, VMEM, VMEM],
     )
     return call(sum_kernel, struct((n_b, width), BF16), swap(sent, "ctx"), specs=[VMEM])

time: 98.1 us -> 97.1 us (0.990)
  blocking collectives: 91.5 us -> 90 us
    all_to_all x5, blocking collectives: 91.5 us -> 90 us  [swap(): return lax.all_to_all(x, axes, split_axis=0, concat_axis=0, tiled=True)]
where the time goes in v3:
time: 97.1 us; the launch traced here: 96.8 us
  blocking collectives  90 us (93%)
  Pallas kernels  6.68 us (7%)
    all_to_all x5, blocking collectives, swap(): return lax.all_to_all(x, axes, split_axis=0, concat_axis=0, tiled=True)  90 us
    pallas_call x6, Pallas kernels, call(): pl.pallas_call(kernel, out_shape=outs, in_specs=specs, out_specs=jax.tree...  6.68 us

profile of v3, /device:TPU:1, one launch (start us, length us, event | category | flops | bytes accessed | tf_op | source)
XLA Modules:
  0.0 96.8 jit_solution(7250842105238469281)
XLA Ops:
  0.0 0.0 copy-start.4
  0.0 2.2 %shard_map.100 = bf16[16,40,128]{2,1,0:T(8,128)(2,1)} custom-call(bf16[4,128,128]{2,1,0:T(8,128)(2,1)} %bitcast.19, bf16[24,128]{1,0:T(8,128)(2,1)} %bitcast.21, s32[4]{0:T(128)} %len_hbm.1, bf16[4,128,128]{2,1,0:T(8,128)(2,1)} %bitcast.20), custom_call_target="tpu_custom_call" | custom-call | flops 68719476736 | bytes 268435456 | tf_op jit(solution)/shard_map/pallas_call | solution.py:25
  2.2 28.0 %all_to_all.25.got_ref = bf16[16,40,128]{2,1,0:T(8,128)(2,1)S(1)} all-to-all(bf16[16,40,128]{2,1,0:T(8,128)(2,1)} %shard_map.100), channel_id=1, replica_groups=mesh['rows'=4,'ctx'=16,'expert'=8] {'ctx'}, dimensions={0} | all-to-all | bytes 327680 | tf_op jit(solution)/shard_map/all_to_all | solution.py:283
  30.2 0.0 copy-done.4
  30.2 1.4 %shard_map.101 = bf16[16,2,128]{2,1,0:T(2,128)(2,1)S(1)} custom-call(bf16[16,40,128]{2,1,0:T(8,128)(2,1)S(1)} %all_to_all.25.got_ref, bf16[4,768]{1,0:T(4,128)(2,1)S(1)} %copy-done.4), custom_call_target="tpu_custom_call" | custom-call | flops 68719476736 | bytes 268435456 | tf_op jit(solution)/shard_map/pallas_call | solution.py:25
  31.7 18.8 %all_to_all.26.got_ref = bf16[16,2,128]{2,1,0:T(2,128)(2,1)S(1)} all-to-all(bf16[16,2,128]{2,1,0:T(2,128)(2,1)S(1)} %shard_map.101), channel_id=1, replica_groups=mesh['rows'=4,'ctx'=16,'expert'=8] {'ctx'}, dimensions={0} | all-to-all | bytes 16384 | tf_op jit(solution)/shard_map/all_to_all | solution.py:283
  50.5 0.0 copy-start
  50.5 0.0 copy-start.1
  50.5 0.0 copy-start.2
  50.5 0.0 copy-start.3
  50.5 0.0 copy-start.5
  50.5 0.2 shard_map.102
  50.8 17.5 %all_to_all.27 = bf16[32,24,128]{2,1,0:T(8,128)(2,1)S(1)} all-to-all(bf16[32,24,128]{2,1,0:T(8,128)(2,1)S(1)} %get-tuple-element.9), channel_id=1, replica_groups=mesh['rows'=4,'ctx'=16,'expert'=8] {'rows','expert'}, dimensions={0} | all-to-all | bytes 393216 | tf_op jit(solution)/shard_map/all_to_all | solution.py:283
  68.2 0.0 copy-done
  68.2 0.0 copy-done.1
  68.3 0.0 copy-done.2
  68.3 0.0 copy-done.3
  68.3 0.0 copy-done.5
  68.3 1.9 %shard_map.103 = (bf16[4,8,24,128]{3,2,1,0:T(8,128)(2,1)S(1)}, f32[24,8]{1,0:T(8,128)S(1)}) custom-call(s32[2,4]{1,0:T(2,128)S(1)} %bitcast.18, bf16[4,192,128]{2,1,0:T(8,128)(2,1)S(1)} %bitcast.12, f32[8,3072]{1,0:T(8,128)S(1)} %bitcast.17, bf16[3072,256]{1,0:T(8,128)(2,1)S(1)} %bitcast.14, bf16[3072,256]{1,0:T(8,128)(2,1)S(1)} %bitcast.15, ...), custom_call_target="tpu_custom_call" | custom-call | flops 68719476736 | bytes 268435456 | tf_op jit(solution)/shard_map/pallas_call | solution.py:25
  70.2 11.9 %all_to_all.28.parts_ref = bf16[32,24,128]{2,1,0:T(8,128)(2,1)S(1)} all-to-all(bf16[32,24,128]{2,1,0:T(8,128)(2,1)S(1)} %bitcast.13), channel_id=1, replica_groups=mesh['rows'=4,'ctx'=16,'expert'=8] {'rows','expert'}, dimensions={0} | all-to-all | bytes 393216 | tf_op jit(solution)/shard_map/all_to_all | solution.py:283
  82.1 0.2 shard_map.104
  82.3 13.8 %all_to_all.29.parts_ref = f32[16,2,96]{2,1,0:T(2,128)S(1)} all-to-all(f32[16,2,96]{2,1,0:T(2,128)S(1)} %shard_map.104), channel_id=1, replica_groups=mesh['rows'=4,'ctx'=16,'expert'=8] {'ctx'}, dimensions={0} | all-to-all | bytes 24576 | tf_op jit(solution)/shard_map/all_to_all | solution.py:283
  96.1 0.7 shard_map.105
Async XLA Ops:
  0.0 30.2 %copy-start.4 = (bf16[4,768]{1,0:T(4,128)(2,1)S(1)}, bf16[4,768]{1,0:T(4,128)(2,1)}, u32[]{:S(2)}) copy-start(bf16[4,768]{1,0:T(4,128)(2,1)} %res_ref.1) | copy-start | bytes 18436
  50.5 17.7 %copy-start = (bf16[1,3072,256]{2,1,0:T(8,128)(2,1)S(1)}, bf16[1,3072,256]{2,1,0:T(8,128)(2,1)}, u32[]{:S(2)}) copy-start(bf16[1,3072,256]{2,1,0:T(8,128)(2,1)} %param.17) | copy-start | bytes 4718596
  50.5 17.7 %copy-start.1 = (bf16[1,3072,256]{2,1,0:T(8,128)(2,1)S(1)}, bf16[1,3072,256]{2,1,0:T(8,128)(2,1)}, u32[]{:S(2)}) copy-start(bf16[1,3072,256]{2,1,0:T(8,128)(2,1)} %param.18) | copy-start | bytes 4718596
  50.5 17.7 %copy-start.2 = (bf16[1,256,3072]{2,1,0:T(8,128)(2,1)S(1)}, bf16[1,256,3072]{2,1,0:T(8,128)(2,1)}, u32[]{:S(2)}) copy-start(bf16[1,256,3072]{2,1,0:T(8,128)(2,1)} %param.19) | copy-start | bytes 4718596
  50.5 17.7 %copy-start.3 = (f32[3072,8]{0,1:T(8,128)S(1)}, f32[3072,8]{0,1:T(8,128)}, u32[]{:S(2)}) copy-start(f32[3072,8]{0,1:T(8,128)} %param.16) | copy-start | bytes 294916
  50.5 17.8 %copy-start.5 = (s32[4,2]{0,1:T(2,128)S(1)}, s32[4,2]{0,1:T(2,128)}, u32[]{:S(2)}) copy-start(s32[4,2]{0,1:T(2,128)} %param.15) | copy-start | bytes 100

commit v4 on v3

--- a/solution.py
+++ b/solution.py
@@ -15,8 +15,8 @@
 BF16 = jnp.bfloat16
 NEG = -1e30
 FAR = 1.25
-SCALE = 143.0
-SHIFT = 80.0
+SCALE = 206.0
+SHIFT = 115.0
 HBM = pl.BlockSpec(memory_space=pltpu.HBM)
 NT = (((1,), (1,)), ((), ()))
 
@@ -79,8 +79,8 @@
         fine = top - coarse
         fine = (fine + jnp.abs(fine) * (1.0 / 128.0)).astype(BF16).astype(F32)
         below = jnp.where(valid, jnp.minimum((coarse + fine) - scaled, FAR), FAR)
-        coded = jnp.exp(SCALE * jnp.sqrt(jnp.maximum(below, 0.0)) - SHIFT)
-        count = jnp.sum(jnp.where(valid, 1.0, 0.0)[0:1], axis=-1, keepdims=True)
+        coded = jnp.exp2(SCALE * jnp.sqrt(jnp.maximum(below, 0.0)) - SHIFT)
+        count = jnp.minimum(jnp.maximum(len_ref[b] - c * here, 0), here).astype(F32)
         tops = [jnp.sum(jnp.where(diagonal, part, 0.0), axis=0, keepdims=True) for part in (coarse, fine)]
         lane = iota((1, here), 1)
         tops[0] = jnp.where(lane < 8, tops[0], count)
@@ -104,11 +104,18 @@
     n_c, rows, here = got_ref.shape
     dims = rows - 8
     b, j = lax.axis_index("ctx") // split, lax.axis_index("ctx") % split
+    row = jnp.dot(one_hot(iota((8, res_ref.shape[0]), 1) == b), res_ref[...], preferred_element_type=F32)
+    res = row[:, 0:here]
+    for h in range(1, heads):
+        res = jnp.where(iota(res.shape, 0) == h, row[:, h * here:(h + 1) * here], res)
+    mine = res[:, 0:dims]
+    for k in range(1, split):
+        mine = jnp.where(j == k, res[:, k * dims:(k + 1) * dims], mine)
     parts = got_ref[:, dims:].astype(F32)
     diagonal = iota((n_c, 8, here), 1) == iota((n_c, 8, here), 2)
     tops = parts[:, heads:heads + 1] + parts[:, heads + 1:heads + 2]
     tops = jnp.sum(jnp.where(diagonal, tops, 0.0), axis=-1, keepdims=True)
-    root = (jnp.log(parts) + SHIFT) * (1.0 / SCALE)
+    root = (jnp.log2(parts) + SHIFT) * (1.0 / SCALE)
     scores = jnp.where(iota(root.shape, 1) < heads, tops - root * root, NEG)
     count = jnp.sum(parts[:, heads:heads + 1, 8:9], axis=0)
     top = jnp.max(jnp.max(scores, axis=0), axis=-1, keepdims=True)
@@ -140,13 +147,6 @@
     weights = jnp.concatenate([weights[i] for i in range(n_c)], axis=1).astype(BF16)
     values = jnp.concatenate([got_ref[i, 0:dims] for i in range(n_c)], axis=1)
     attended = lax.dot_general(weights, values, NT, preferred_element_type=F32) / total
-    res = res_ref[...].astype(F32)
-    res = jnp.sum(jnp.where(iota(res.shape, 0) == b, res, 0.0), axis=0, keepdims=True)
-    res = [res[:, h * here:(h + 1) * here] for h in range(heads)]
-    res = jnp.concatenate(res + [jnp.zeros((8 - heads, here), F32)], axis=0)
-    mine = res[:, 0:dims]
-    for k in range(1, split):
-        mine = jnp.where(j == k, res[:, k * dims:(k + 1) * dims], mine)
     hidden = mine + attended
     flat = [hidden[h:h + 1] for h in range(heads)]
     flat += [jnp.zeros((1, dims), F32)] * (-heads % split)

time: 97.1 us -> 97.1 us (level)
  no operation moved by 1% of the time
where the time goes in v4:
time: 97.1 us; the launch traced here: 96.8 us
  blocking collectives  90 us (93%)
  Pallas kernels  6.71 us (7%)
    all_to_all x5, blocking collectives, swap(): return lax.all_to_all(x, axes, split_axis=0, concat_axis=0, tiled=True)  90 us
    pallas_call x6, Pallas kernels, call(): pl.pallas_call(kernel, out_shape=outs, in_specs=specs, out_specs=jax.tree...  6.71 us

profile of v4, /device:TPU:1, one launch (start us, length us, event | category | flops | bytes accessed | tf_op | source)
XLA Modules:
  0.0 96.8 jit_solution(8795607660190701498)
XLA Ops:
  0.0 0.0 copy-start.4
  0.0 2.2 %shard_map.100 = bf16[16,40,128]{2,1,0:T(8,128)(2,1)} custom-call(bf16[4,128,128]{2,1,0:T(8,128)(2,1)} %bitcast.19, bf16[24,128]{1,0:T(8,128)(2,1)} %bitcast.21, s32[4]{0:T(128)} %len_hbm.1, bf16[4,128,128]{2,1,0:T(8,128)(2,1)} %bitcast.20), custom_call_target="tpu_custom_call" | custom-call | flops 68719476736 | bytes 268435456 | tf_op jit(solution)/shard_map/pallas_call | solution.py:25
  2.2 28.0 %all_to_all.25.got_ref = bf16[16,40,128]{2,1,0:T(8,128)(2,1)S(1)} all-to-all(bf16[16,40,128]{2,1,0:T(8,128)(2,1)} %shard_map.100), channel_id=1, replica_groups=mesh['rows'=4,'ctx'=16,'expert'=8] {'ctx'}, dimensions={0} | all-to-all | bytes 327680 | tf_op jit(solution)/shard_map/all_to_all | solution.py:283
  30.2 0.0 copy-done.4
  30.2 1.5 %shard_map.101 = bf16[16,2,128]{2,1,0:T(2,128)(2,1)S(1)} custom-call(bf16[16,40,128]{2,1,0:T(8,128)(2,1)S(1)} %all_to_all.25.got_ref, bf16[4,768]{1,0:T(4,128)(2,1)S(1)} %copy-done.4), custom_call_target="tpu_custom_call" | custom-call | flops 68719476736 | bytes 268435456 | tf_op jit(solution)/shard_map/pallas_call | solution.py:25
  31.7 18.6 %all_to_all.26.got_ref = bf16[16,2,128]{2,1,0:T(2,128)(2,1)S(1)} all-to-all(bf16[16,2,128]{2,1,0:T(2,128)(2,1)S(1)} %shard_map.101), channel_id=1, replica_groups=mesh['rows'=4,'ctx'=16,'expert'=8] {'ctx'}, dimensions={0} | all-to-all | bytes 16384 | tf_op jit(solution)/shard_map/all_to_all | solution.py:283
  50.3 0.0 copy-start
  50.3 0.0 copy-start.1
  50.3 0.0 copy-start.2
  50.3 0.0 copy-start.3
  50.3 0.0 copy-start.5
  50.3 0.2 shard_map.102
  50.6 17.7 %all_to_all.27 = bf16[32,24,128]{2,1,0:T(8,128)(2,1)S(1)} all-to-all(bf16[32,24,128]{2,1,0:T(8,128)(2,1)S(1)} %get-tuple-element.9), channel_id=1, replica_groups=mesh['rows'=4,'ctx'=16,'expert'=8] {'rows','expert'}, dimensions={0} | all-to-all | bytes 393216 | tf_op jit(solution)/shard_map/all_to_all | solution.py:283
  68.3 0.0 copy-done
  68.3 0.0 copy-done.1
  68.3 0.0 copy-done.2
  68.3 0.0 copy-done.3
  68.3 0.0 copy-done.5
  68.3 1.9 %shard_map.103 = (bf16[4,8,24,128]{3,2,1,0:T(8,128)(2,1)S(1)}, f32[24,8]{1,0:T(8,128)S(1)}) custom-call(s32[2,4]{1,0:T(2,128)S(1)} %bitcast.18, bf16[4,192,128]{2,1,0:T(8,128)(2,1)S(1)} %bitcast.12, f32[8,3072]{1,0:T(8,128)S(1)} %bitcast.17, bf16[3072,256]{1,0:T(8,128)(2,1)S(1)} %bitcast.14, bf16[3072,256]{1,0:T(8,128)(2,1)S(1)} %bitcast.15, ...), custom_call_target="tpu_custom_call" | custom-call | flops 68719476736 | bytes 268435456 | tf_op jit(solution)/shard_map/pallas_call | solution.py:25
  70.2 11.9 %all_to_all.28.parts_ref = bf16[32,24,128]{2,1,0:T(8,128)(2,1)S(1)} all-to-all(bf16[32,24,128]{2,1,0:T(8,128)(2,1)S(1)} %bitcast.13), channel_id=1, replica_groups=mesh['rows'=4,'ctx'=16,'expert'=8] {'rows','expert'}, dimensions={0} | all-to-all | bytes 393216 | tf_op jit(solution)/shard_map/all_to_all | solution.py:283
  82.1 0.2 shard_map.104
  82.3 13.8 %all_to_all.29.parts_ref = f32[16,2,96]{2,1,0:T(2,128)S(1)} all-to-all(f32[16,2,96]{2,1,0:T(2,128)S(1)} %shard_map.104), channel_id=1, replica_groups=mesh['rows'=4,'ctx'=16,'expert'=8] {'ctx'}, dimensions={0} | all-to-all | bytes 24576 | tf_op jit(solution)/shard_map/all_to_all | solution.py:283
  96.1 0.7 shard_map.105
Async XLA Ops:
  0.0 30.2 %copy-start.4 = (bf16[4,768]{1,0:T(4,128)(2,1)S(1)}, bf16[4,768]{1,0:T(4,128)(2,1)}, u32[]{:S(2)}) copy-start(bf16[4,768]{1,0:T(4,128)(2,1)} %res_ref.1) | copy-start | bytes 18436
  50.3 18.0 %copy-start = (bf16[1,3072,256]{2,1,0:T(8,128)(2,1)S(1)}, bf16[1,3072,256]{2,1,0:T(8,128)(2,1)}, u32[]{:S(2)}) copy-start(bf16[1,3072,256]{2,1,0:T(8,128)(2,1)} %param.17) | copy-start | bytes 4718596
  50.3 18.0 %copy-start.1 = (bf16[1,3072,256]{2,1,0:T(8,128)(2,1)S(1)}, bf16[1,3072,256]{2,1,0:T(8,128)(2,1)}, u32[]{:S(2)}) copy-start(bf16[1,3072,256]{2,1,0:T(8,128)(2,1)} %param.18) | copy-start | bytes 4718596
  50.3 18.0 %copy-start.2 = (bf16[1,256,3072]{2,1,0:T(8,128)(2,1)S(1)}, bf16[1,256,3072]{2,1,0:T(8,128)(2,1)}, u32[]{:S(2)}) copy-start(bf16[1,256,3072]{2,1,0:T(8,128)(2,1)} %param.19) | copy-start | bytes 4718596
  50.3 18.0 %copy-start.3 = (f32[3072,8]{0,1:T(8,128)S(1)}, f32[3072,8]{0,1:T(8,128)}, u32[]{:S(2)}) copy-start(f32[3072,8]{0,1:T(8,128)} %param.16) | copy-start | bytes 294916
  50.3 18.0 %copy-start.5 = (s32[4,2]{0,1:T(2,128)S(1)}, s32[4,2]{0,1:T(2,128)}, u32[]{:S(2)}) copy-start(s32[4,2]{0,1:T(2,128)} %param.15) | copy-start | bytes 100

commit v5 on v4

--- a/solution.py
+++ b/solution.py
@@ -66,10 +66,10 @@
     diagonal = iota((8, here), 0) == iota((8, here), 1)
     at, src = iota((8 * n_b, heads * n_b), 0), iota((8 * n_b, heads * n_b), 1)
     pick = one_hot(src == at % 8 * n_b + at // 8)
-    for copy in copies[:3]:
+    for copy in copies:
         copy.wait()
     q = jnp.dot(pick, q_ref[...], preferred_element_type=F32)
-    tails = []
+    out_copies = []
     for b in range(n_b):
         q_b = q[8 * b:8 * b + 8].astype(BF16)
         scaled = lax.dot_general(q_b, k_ref[b], NT, preferred_element_type=F32) * (0.5 / math.sqrt(size))
@@ -85,13 +85,10 @@
         lane = iota((1, here), 1)
         tops[0] = jnp.where(lane < 8, tops[0], count)
         rows = [coded[0:heads]] + tops
-        tails.append(jnp.concatenate(rows, axis=0))
-    copies[3].wait()
-    out_copies = []
-    for b in range(n_b):
+        tail = jnp.concatenate(rows, axis=0)
         turned = lax.dot_general(eye, v_ref[b], NT, preferred_element_type=F32)
         for j in range(split):
-            block = jnp.concatenate([turned[j * dims:(j + 1) * dims], tails[b]], axis=0)
+            block = jnp.concatenate([turned[j * dims:(j + 1) * dims], tail], axis=0)
             out_ref[b * split + j] = block.astype(BF16)
         cut = pl.ds(b * split, split)
         out_copies.append(pltpu.make_async_copy(out_ref.at[cut], out_hbm.at[cut], out_sems.at[b]))

time: 97.1 us -> 97 us (level)
  no operation moved by 1% of the time
where the time goes in v5:
time: 97 us; the launch traced here: 96.7 us
  blocking collectives  90 us (93%)
  Pallas kernels  6.62 us (7%)
    all_to_all x5, blocking collectives, swap(): return lax.all_to_all(x, axes, split_axis=0, concat_axis=0, tiled=True)  90 us
    pallas_call x6, Pallas kernels, call(): pl.pallas_call(kernel, out_shape=outs, in_specs=specs, out_specs=jax.tree...  6.62 us

profile of v5, /device:TPU:1, one launch (start us, length us, event | category | flops | bytes accessed | tf_op | source)
XLA Modules:
  0.0 96.7 jit_solution(9987868142739739720)
XLA Ops:
  0.0 0.0 copy-start.4
  0.0 2.1 %shard_map.100 = bf16[16,40,128]{2,1,0:T(8,128)(2,1)} custom-call(bf16[4,128,128]{2,1,0:T(8,128)(2,1)} %bitcast.19, bf16[24,128]{1,0:T(8,128)(2,1)} %bitcast.21, s32[4]{0:T(128)} %len_hbm.1, bf16[4,128,128]{2,1,0:T(8,128)(2,1)} %bitcast.20), custom_call_target="tpu_custom_call" | custom-call | flops 68719476736 | bytes 268435456 | tf_op jit(solution)/shard_map/pallas_call | solution.py:25
  2.1 28.0 %all_to_all.25.got_ref = bf16[16,40,128]{2,1,0:T(8,128)(2,1)S(1)} all-to-all(bf16[16,40,128]{2,1,0:T(8,128)(2,1)} %shard_map.100), channel_id=1, replica_groups=mesh['rows'=4,'ctx'=16,'expert'=8] {'ctx'}, dimensions={0} | all-to-all | bytes 327680 | tf_op jit(solution)/shard_map/all_to_all | solution.py:280
  30.1 0.0 copy-done.4
  30.1 1.5 %shard_map.101 = bf16[16,2,128]{2,1,0:T(2,128)(2,1)S(1)} custom-call(bf16[16,40,128]{2,1,0:T(8,128)(2,1)S(1)} %all_to_all.25.got_ref, bf16[4,768]{1,0:T(4,128)(2,1)S(1)} %copy-done.4), custom_call_target="tpu_custom_call" | custom-call | flops 68719476736 | bytes 268435456 | tf_op jit(solution)/shard_map/pallas_call | solution.py:25
  31.6 18.8 %all_to_all.26.got_ref = bf16[16,2,128]{2,1,0:T(2,128)(2,1)S(1)} all-to-all(bf16[16,2,128]{2,1,0:T(2,128)(2,1)S(1)} %shard_map.101), channel_id=1, replica_groups=mesh['rows'=4,'ctx'=16,'expert'=8] {'ctx'}, dimensions={0} | all-to-all | bytes 16384 | tf_op jit(solution)/shard_map/all_to_all | solution.py:280
  50.4 0.0 copy-start
  50.4 0.0 copy-start.1
  50.4 0.0 copy-start.2
  50.4 0.0 copy-start.3
  50.4 0.0 copy-start.5
  50.5 0.2 shard_map.102
  50.7 17.5 %all_to_all.27 = bf16[32,24,128]{2,1,0:T(8,128)(2,1)S(1)} all-to-all(bf16[32,24,128]{2,1,0:T(8,128)(2,1)S(1)} %get-tuple-element.9), channel_id=1, replica_groups=mesh['rows'=4,'ctx'=16,'expert'=8] {'rows','expert'}, dimensions={0} | all-to-all | bytes 393216 | tf_op jit(solution)/shard_map/all_to_all | solution.py:280
  68.2 0.0 copy-done
  68.2 0.0 copy-done.1
  68.2 0.0 copy-done.2
  68.2 0.0 copy-done.3
  68.2 0.0 copy-done.5
  68.2 1.9 %shard_map.103 = (bf16[4,8,24,128]{3,2,1,0:T(8,128)(2,1)S(1)}, f32[24,8]{1,0:T(8,128)S(1)}) custom-call(s32[2,4]{1,0:T(2,128)S(1)} %bitcast.18, bf16[4,192,128]{2,1,0:T(8,128)(2,1)S(1)} %bitcast.12, f32[8,3072]{1,0:T(8,128)S(1)} %bitcast.17, bf16[3072,256]{1,0:T(8,128)(2,1)S(1)} %bitcast.14, bf16[3072,256]{1,0:T(8,128)(2,1)S(1)} %bitcast.15, ...), custom_call_target="tpu_custom_call" | custom-call | flops 68719476736 | bytes 268435456 | tf_op jit(solution)/shard_map/pallas_call | solution.py:25
  70.1 11.9 %all_to_all.28.parts_ref = bf16[32,24,128]{2,1,0:T(8,128)(2,1)S(1)} all-to-all(bf16[32,24,128]{2,1,0:T(8,128)(2,1)S(1)} %bitcast.13), channel_id=1, replica_groups=mesh['rows'=4,'ctx'=16,'expert'=8] {'rows','expert'}, dimensions={0} | all-to-all | bytes 393216 | tf_op jit(solution)/shard_map/all_to_all | solution.py:280
  82.0 0.2 shard_map.104
  82.2 13.8 %all_to_all.29.parts_ref = f32[16,2,96]{2,1,0:T(2,128)S(1)} all-to-all(f32[16,2,96]{2,1,0:T(2,128)S(1)} %shard_map.104), channel_id=1, replica_groups=mesh['rows'=4,'ctx'=16,'expert'=8] {'ctx'}, dimensions={0} | all-to-all | bytes 24576 | tf_op jit(solution)/shard_map/all_to_all | solution.py:280
  96.0 0.7 shard_map.105
Async XLA Ops:
  0.0 30.1 %copy-start.4 = (bf16[4,768]{1,0:T(4,128)(2,1)S(1)}, bf16[4,768]{1,0:T(4,128)(2,1)}, u32[]{:S(2)}) copy-start(bf16[4,768]{1,0:T(4,128)(2,1)} %res_ref.1) | copy-start | bytes 18436
  50.4 17.8 %copy-start = (bf16[1,3072,256]{2,1,0:T(8,128)(2,1)S(1)}, bf16[1,3072,256]{2,1,0:T(8,128)(2,1)}, u32[]{:S(2)}) copy-start(bf16[1,3072,256]{2,1,0:T(8,128)(2,1)} %param.17) | copy-start | bytes 4718596
  50.4 17.8 %copy-start.1 = (bf16[1,3072,256]{2,1,0:T(8,128)(2,1)S(1)}, bf16[1,3072,256]{2,1,0:T(8,128)(2,1)}, u32[]{:S(2)}) copy-start(bf16[1,3072,256]{2,1,0:T(8,128)(2,1)} %param.18) | copy-start | bytes 4718596
  50.4 17.8 %copy-start.2 = (bf16[1,256,3072]{2,1,0:T(8,128)(2,1)S(1)}, bf16[1,256,3072]{2,1,0:T(8,128)(2,1)}, u32[]{:S(2)}) copy-start(bf16[1,256,3072]{2,1,0:T(8,128)(2,1)} %param.19) | copy-start | bytes 4718596
  50.4 17.8 %copy-start.3 = (f32[3072,8]{0,1:T(8,128)S(1)}, f32[3072,8]{0,1:T(8,128)}, u32[]{:S(2)}) copy-start(f32[3072,8]{0,1:T(8,128)} %param.16) | copy-start | bytes 294916
  50.4 17.8 %copy-start.5 = (s32[4,2]{0,1:T(2,128)S(1)}, s32[4,2]{0,1:T(2,128)}, u32[]{:S(2)}) copy-start(s32[4,2]{0,1:T(2,128)} %param.15) | copy-start | bytes 100
